TPU v7x, 32 devices: a whole 2x2x4 slice. The times are simulated.
32 devices in a mesh: seq: 4 (over x, core), blk: 8 (over z, y).
Axes of the slice: x: 2, y: 2, z: 4, core: 2. Of those that a mesh axis runs over, the one named last changes fastest.
Arguments:
- tokens: bfloat16 [4, 128, 16, 1152], P('seq', 'blk'), may hold values from -6 to 6
- segments: int32 [4, 16], P('seq'), may hold values from 0 to 1, never falling along the last dimension, each value on 1 to 9 neighbouring positions
- timesteps: int32 [4, 2], P('seq'), may hold values from 0 to 999
- caption: bfloat16 [4, 2, 120, 4096], P('seq'), may hold values from -6 to 6
- cotangent: bfloat16 [4, 128, 16, 1152], P('seq', 'blk'), may hold values from -6 to 6
- ada_weight: bfloat16 [1152, 10368], P(None, 'blk'), may hold values from -0.1875 to 0.1875
- ada_bias: bfloat16 [10368], P('blk'), may hold values from -3 to 3
- spatial_in: bfloat16 [1152, 3456], P(('seq', 'blk')), may hold values from -0.1875 to 0.1875
- spatial_out: bfloat16 [1152, 1152], P(('seq', 'blk')), may hold values from -1 to 1
- temporal_in: bfloat16 [1152, 3456], P(('seq', 'blk')), may hold values from -0.1875 to 0.1875
- temporal_out: bfloat16 [1152, 1152], P(('seq', 'blk')), may hold values from -0.5 to 0.5
- cross_gain: bfloat16 [1152], P(('seq', 'blk')), may hold values from 0.25 to 1.75
- cross_query: bfloat16 [1152, 1152], P(('seq', 'blk')), may hold values from -0.1875 to 0.1875
- caption_proj: bfloat16 [4096, 2304], P(None, 'blk'), may hold values from -0.09375 to 0.09375
- cross_out: bfloat16 [1152, 1152], P(('seq', 'blk')), may hold values from -1.25 to 1.25
- hidden_in: bfloat16 [1152, 4608], P(('seq', 'blk')), may hold values from -0.1875 to 0.1875
- hidden_out: bfloat16 [4608, 1152], P(('seq', 'blk')), may hold values from -0.09375 to 0.09375
Outputs:
- out: bfloat16 [4, 128, 16, 1152], P('seq', 'blk')
- grad_tokens: bfloat16 [4, 128, 16, 1152], P('seq', 'blk')
- grad_ada_weight: float32 [1152, 10368], P(None, 'blk')
- grad_ada_bias: float32 [10368], P('blk')
- grad_spatial_in: float32 [1152, 3456], P(('seq', 'blk'))
- grad_spatial_out: float32 [1152, 1152], P(('seq', 'blk'))
- grad_temporal_in: float32 [1152, 3456], P(('seq', 'blk'))
- grad_temporal_out: float32 [1152, 1152], P(('seq', 'blk'))
- grad_cross_gain: float32 [1152], P(('seq', 'blk'))
- grad_cross_query: float32 [1152, 1152], P(('seq', 'blk'))
- grad_caption_proj: float32 [4096, 2304], P(None, 'blk')
- grad_cross_out: float32 [1152, 1152], P(('seq', 'blk'))
- grad_hidden_in: float32 [1152, 4608], P(('seq', 'blk'))
- grad_hidden_out: float32 [4608, 1152], P(('seq', 'blk'))
Inputs may be any that keep to these rules, and one draw needn't show every extreme that they name: `segments`: along the 16 frames of a pack the video number never falls; each of the 2 videos holds at least 7 and at most 9 frames.
All inputs are finite; a program needn't handle non-finite values.
Results may differ from a plain program's by a relative error of at most 0.035.
Values may be sent and summed in bfloat16 or wider, within the bound.
A program may use at most 384 MiB of HBM per device.

v0:
```python
import math

import jax
import jax.numpy as jnp
import numpy as np
from jax import lax
from jax.experimental import pallas as pl
from jax.experimental.pallas import tpu as pltpu
from jax.sharding import PartitionSpec as P

H = 16
E = 72
L = 120


EPSILON = 1e-06
MASKED = -1e30


def to_low(values):
    return values.astype(jnp.bfloat16)


def linear(left, right):
    return jnp.dot(left, right, preferred_element_type=jnp.float32)


def left_product(left, right):
    return lax.dot_general(
        left, right, (((0,), (0,)), ((), ())), preferred_element_type=jnp.float32
    )


def right_product(left, right):
    return lax.dot_general(
        left, right, (((1,), (1,)), ((), ())), preferred_element_type=jnp.float32
    )


def normalize(values):
    center = values - jnp.mean(values, axis=-1, keepdims=True)
    return center * lax.rsqrt(jnp.mean(center * center, axis=-1, keepdims=True) + EPSILON)


def modulate(values, shift_rows, scale_rows):
    return normalize(values) * (1.0 + scale_rows) + shift_rows


def gain_norm(values, gain_row):
    return normalize(values) * gain_row


def gelu_tanh(values):
    return jax.nn.gelu(values, approximate=True)


def softmax_rows(scores):
    shifted = jnp.exp(scores - jnp.max(scores, axis=-1, keepdims=True))
    return shifted / jnp.sum(shifted, axis=-1, keepdims=True)


def softmax_with_total(scores):
    top = jnp.max(scores, axis=-1, keepdims=True)
    shifted = jnp.exp(scores - top)
    total = jnp.sum(shifted, axis=-1, keepdims=True)
    return (shifted / total, (top + jnp.log(total))[..., 0])


def softmax_back(probs, grad_probs):
    return probs * (grad_probs - jnp.sum(grad_probs * probs, axis=-1, keepdims=True))


def time_embedding(step_ids, model_width):
    half_width = model_width // 2
    frequency = jnp.exp(
        -math.log(10000.0) * jnp.arange(half_width).astype(jnp.float32) / half_width
    )
    angles = step_ids.astype(jnp.float32)[:, None] * frequency[None, :]
    return jnp.concatenate([jnp.cos(angles), jnp.sin(angles)], axis=1)


def general_shards(
    tokens,
    segments,
    timesteps,
    caption,
    cotangent,
    ada_weight,
    ada_bias,
    spatial_in,
    spatial_out,
    temporal_in,
    temporal_out,
    cross_gain,
    cross_query,
    caption_proj,
    cross_out,
    hidden_in,
    hidden_out,
):
    inputs = tokens[0].astype(jnp.float32)
    patch_dev, frames, model_width = inputs.shape
    token_rows = patch_dev * frames
    head_count = H
    head_size = E
    score_scale = E ** (-0.5)
    frame_seg = segments[0]
    step_ids = timesteps[0]
    seg_count, text_len, text_width = caption.shape[1:]
    text_keys = seg_count * text_len
    caption_rows = caption[0].reshape(text_keys, text_width)
    grad_out = cotangent[0].astype(jnp.float32)
    gathered = (
        lax.all_gather(spatial_in, ("seq", "blk"), axis=0, tiled=True),
        lax.all_gather(spatial_out, ("seq", "blk"), axis=0, tiled=True),
        lax.all_gather(temporal_in, ("seq", "blk"), axis=0, tiled=True),
        lax.all_gather(temporal_out, ("seq", "blk"), axis=0, tiled=True),
        lax.all_gather(cross_gain, ("seq", "blk"), axis=0, tiled=True),
        lax.all_gather(cross_query, ("seq", "blk"), axis=0, tiled=True),
        lax.all_gather(cross_out, ("seq", "blk"), axis=0, tiled=True),
        lax.all_gather(hidden_in, ("seq", "blk"), axis=0, tiled=True),
        lax.all_gather(hidden_out, ("seq", "blk"), axis=0, tiled=True),
    )
    (
        wide_sin,
        wide_sout,
        wide_tin,
        wide_tout,
        gain_low,
        wide_query,
        wide_cout,
        wide_hin,
        wide_hout,
    ) = gathered
    gain_row = gain_low.astype(jnp.float32)
    conditioning = to_low(jax.nn.silu(time_embedding(step_ids, model_width)))
    mod_part = to_low(linear(conditioning, ada_weight) + ada_bias.astype(jnp.float32))
    text_part = to_low(linear(caption_rows, caption_proj))
    modulation, memory = (
        lax.all_gather(mod_part, "blk", axis=1, tiled=True),
        lax.all_gather(text_part, "blk", axis=1, tiled=True),
    )
    choose = frame_seg[:, None] == jnp.arange(seg_count, dtype=jnp.int32)[None, :]
    frame_mod = linear(choose.astype(jnp.bfloat16), modulation)
    pieces = [frame_mod[:, index * model_width : (index + 1) * model_width] for index in range(9)]
    (
        shift_one,
        scale_one,
        gate_one,
        shift_two,
        scale_two,
        gate_two,
        shift_three,
        scale_three,
        gate_three,
    ) = pieces
    spatial_input = to_low(modulate(inputs, shift_one, scale_one)).reshape(token_rows, model_width)
    spatial_qkv = to_low(linear(spatial_input, wide_sin)).reshape(
        patch_dev, frames, 3 * model_width
    )
    query_s = spatial_qkv[..., :model_width].reshape(patch_dev, frames, head_count, head_size)
    local_kv = spatial_qkv[..., model_width:]
    whole_kv = lax.all_gather(local_kv, "blk", axis=0, tiled=True)

    def split_kv(both):
        count = both.shape[0]
        return (
            both[..., :model_width].reshape(count, frames, head_count, head_size),
            both[..., model_width:].reshape(count, frames, head_count, head_size),
        )

    def spatial_probs(key_all):
        scores = jnp.einsum("pfhe,qfhe->fhpq", query_s, key_all, preferred_element_type=jnp.float32)
        return softmax_with_total(scores * score_scale)

    key_s, value_s = split_kv(whole_kv)
    probs_s, log_total_s = spatial_probs(key_s)
    probs_s_low = to_low(probs_s)
    attn_s = to_low(
        jnp.einsum(
            "fhpq,qfhe->pfhe", probs_s_low, value_s, preferred_element_type=jnp.float32
        ).reshape(token_rows, model_width)
    )
    branch_s = linear(attn_s, wide_sout).reshape(patch_dev, frames, model_width)
    after_one = inputs + gate_one * branch_s
    temporal_input = to_low(modulate(after_one, shift_two, scale_two)).reshape(
        token_rows, model_width
    )
    temporal_qkv = to_low(linear(temporal_input, wide_tin)).reshape(
        patch_dev, frames, 3, head_count, head_size
    )
    query_t = temporal_qkv[:, :, 0]
    key_t = temporal_qkv[:, :, 1]
    value_t = temporal_qkv[:, :, 2]
    same_seg = frame_seg[:, None] == frame_seg[None, :]
    scores_t = (
        jnp.einsum("pfhe,pghe->phfg", query_t, key_t, preferred_element_type=jnp.float32)
        * score_scale
    )
    probs_t = softmax_rows(jnp.where(same_seg[None, None], scores_t, MASKED))
    probs_t_low = to_low(probs_t)
    attn_t = to_low(
        jnp.einsum(
            "phfg,pghe->pfhe", probs_t_low, value_t, preferred_element_type=jnp.float32
        ).reshape(token_rows, model_width)
    )
    branch_t = linear(attn_t, wide_tout).reshape(patch_dev, frames, model_width)
    after_two = after_one + gate_two * branch_t
    cross_input = to_low(gain_norm(after_two, gain_row)).reshape(token_rows, model_width)
    query_c = to_low(linear(cross_input, wide_query)).reshape(
        patch_dev, frames, head_count, head_size
    )
    key_c = memory[:, :model_width].reshape(text_keys, head_count, head_size)
    value_c = memory[:, model_width:].reshape(text_keys, head_count, head_size)
    key_seg = jnp.arange(text_keys, dtype=jnp.int32) // text_len
    allowed = frame_seg[:, None] == key_seg[None, :]
    scores_c = (
        jnp.einsum("pfhe,khe->pfhk", query_c, key_c, preferred_element_type=jnp.float32)
        * score_scale
    )
    probs_c = softmax_rows(jnp.where(allowed[None, :, None, :], scores_c, MASKED))
    probs_c_low = to_low(probs_c)
    attn_c = to_low(
        jnp.einsum(
            "pfhk,khe->pfhe", probs_c_low, value_c, preferred_element_type=jnp.float32
        ).reshape(token_rows, model_width)
    )
    branch_c = linear(attn_c, wide_cout).reshape(patch_dev, frames, model_width)
    after_three = after_two + branch_c
    mlp_input = to_low(modulate(after_three, shift_three, scale_three)).reshape(
        token_rows, model_width
    )
    pre_act = linear(mlp_input, wide_hin)
    post_act = to_low(gelu_tanh(pre_act))
    branch_m = linear(post_act, wide_hout).reshape(patch_dev, frames, model_width)
    result = after_three + gate_three * branch_m
    grad_gate_three = jnp.sum(grad_out * branch_m, axis=0)
    grad_four = to_low(grad_out * gate_three).reshape(token_rows, model_width)
    grad_hout = left_product(post_act, grad_four)
    grad_post = right_product(grad_four, wide_hout)
    gelu_pull = jax.vjp(gelu_tanh, pre_act)[1]
    grad_pre = to_low(gelu_pull(grad_post)[0])
    grad_hin = left_product(mlp_input, grad_pre)
    grad_mlp_in = right_product(grad_pre, wide_hin).reshape(patch_dev, frames, model_width)
    mlp_pull = jax.vjp(modulate, after_three, shift_three, scale_three)[1]
    back_three, grad_shift_three, grad_scale_three = mlp_pull(grad_mlp_in)
    grad_three = grad_out + back_three
    grad_cross_branch = to_low(grad_three).reshape(token_rows, model_width)
    grad_cout = left_product(attn_c, grad_cross_branch)
    grad_attn_c = to_low(right_product(grad_cross_branch, wide_cout)).reshape(
        patch_dev, frames, head_count, head_size
    )
    grad_probs_c = jnp.einsum(
        "pfhe,khe->pfhk", grad_attn_c, value_c, preferred_element_type=jnp.float32
    )
    grad_scores_c = to_low(softmax_back(probs_c, grad_probs_c))
    grad_query_c = to_low(
        jnp.einsum("pfhk,khe->pfhe", grad_scores_c, key_c, preferred_element_type=jnp.float32)
        * score_scale
    ).reshape(token_rows, model_width)
    grad_key_c = (
        jnp.einsum("pfhk,pfhe->khe", grad_scores_c, query_c, preferred_element_type=jnp.float32)
        * score_scale
    )
    grad_value_c = jnp.einsum(
        "pfhk,pfhe->khe", probs_c_low, grad_attn_c, preferred_element_type=jnp.float32
    )
    grad_memory = jnp.concatenate(
        [grad_key_c.reshape(text_keys, model_width), grad_value_c.reshape(text_keys, model_width)],
        axis=1,
    )
    grad_wquery = left_product(cross_input, grad_query_c)
    grad_cross_in = right_product(grad_query_c, wide_query).reshape(patch_dev, frames, model_width)
    cross_pull = jax.vjp(gain_norm, after_two, gain_row)[1]
    back_two, grad_gain = cross_pull(grad_cross_in)
    grad_two = grad_three + back_two
    grad_gate_two = jnp.sum(grad_two * branch_t, axis=0)
    grad_temporal_branch = to_low(grad_two * gate_two).reshape(token_rows, model_width)
    grad_tout = left_product(attn_t, grad_temporal_branch)
    grad_attn_t = to_low(right_product(grad_temporal_branch, wide_tout)).reshape(
        patch_dev, frames, head_count, head_size
    )
    grad_probs_t = jnp.einsum(
        "pfhe,pghe->phfg", grad_attn_t, value_t, preferred_element_type=jnp.float32
    )
    grad_scores_t = to_low(softmax_back(probs_t, grad_probs_t))
    grad_query_t = (
        jnp.einsum("phfg,pghe->pfhe", grad_scores_t, key_t, preferred_element_type=jnp.float32)
        * score_scale
    )
    grad_key_t = (
        jnp.einsum("phfg,pfhe->pghe", grad_scores_t, query_t, preferred_element_type=jnp.float32)
        * score_scale
    )
    grad_value_t = jnp.einsum(
        "phfg,pfhe->pghe", probs_t_low, grad_attn_t, preferred_element_type=jnp.float32
    )
    grad_qkv_t = to_low(jnp.stack([grad_query_t, grad_key_t, grad_value_t], axis=2)).reshape(
        token_rows, 3 * model_width
    )
    grad_tin = left_product(temporal_input, grad_qkv_t)
    grad_temporal_in = right_product(grad_qkv_t, wide_tin).reshape(patch_dev, frames, model_width)
    temporal_pull = jax.vjp(modulate, after_one, shift_two, scale_two)[1]
    back_one, grad_shift_two, grad_scale_two = temporal_pull(grad_temporal_in)
    grad_one = grad_two + back_one
    grad_gate_one = jnp.sum(grad_one * branch_s, axis=0)
    grad_spatial_branch = to_low(grad_one * gate_one).reshape(token_rows, model_width)
    grad_sout = left_product(attn_s, grad_spatial_branch)
    grad_attn_s = to_low(right_product(grad_spatial_branch, wide_sout)).reshape(
        patch_dev, frames, head_count, head_size
    )
    back_kv = lax.all_gather(local_kv, "blk", axis=0, tiled=True)
    back_key, back_value = split_kv(back_kv)
    back_probs = spatial_probs(back_key)[0]
    back_probs_low = to_low(back_probs)
    grad_probs_s = jnp.einsum(
        "pfhe,qfhe->fhpq", grad_attn_s, back_value, preferred_element_type=jnp.float32
    )
    row_delta = jnp.sum(grad_probs_s * back_probs, axis=-1, keepdims=True)
    grad_scores_s = to_low(back_probs * (grad_probs_s - row_delta))
    grad_query_s = (
        jnp.einsum("fhpq,qfhe->pfhe", grad_scores_s, back_key, preferred_element_type=jnp.float32)
        * score_scale
    )
    count = lax.axis_size("blk") * patch_dev
    grad_key = (
        jnp.einsum("fhpq,pfhe->qfhe", grad_scores_s, query_s, preferred_element_type=jnp.float32)
        * score_scale
    )
    grad_value = jnp.einsum(
        "fhpq,pfhe->qfhe", back_probs_low, grad_attn_s, preferred_element_type=jnp.float32
    )
    grad_kv = to_low(
        lax.psum_scatter(
            jnp.concatenate(
                [
                    grad_key.reshape(count, frames, model_width),
                    grad_value.reshape(count, frames, model_width),
                ],
                axis=2,
            ).astype(jnp.bfloat16),
            "blk",
            scatter_dimension=0,
            tiled=True,
        ).astype(jnp.float32)
    )
    grad_qkv_s = jnp.concatenate(
        [to_low(grad_query_s).reshape(patch_dev, frames, model_width), grad_kv], axis=2
    ).reshape(token_rows, 3 * model_width)
    grad_sin = left_product(spatial_input, grad_qkv_s)
    grad_spatial_in = right_product(grad_qkv_s, wide_sin).reshape(patch_dev, frames, model_width)
    spatial_pull = jax.vjp(modulate, inputs, shift_one, scale_one)[1]
    back_zero, grad_shift_one, grad_scale_one = spatial_pull(grad_spatial_in)
    grad_input = grad_one + back_zero
    grad_frame_mod = jnp.concatenate(
        [
            grad_shift_one,
            grad_scale_one,
            grad_gate_one,
            grad_shift_two,
            grad_scale_two,
            grad_gate_two,
            grad_shift_three,
            grad_scale_three,
            grad_gate_three,
        ],
        axis=1,
    )
    grad_mod_local = lax.dot_general(
        choose.astype(jnp.float32),
        grad_frame_mod,
        (((0,), (0,)), ((), ())),
        precision=lax.Precision.HIGHEST,
    )
    grad_mod_part, grad_memory_part = (
        lax.psum_scatter(
            grad_mod_local.astype(jnp.bfloat16), "blk", scatter_dimension=1, tiled=True
        ).astype(jnp.float32),
        lax.psum_scatter(
            grad_memory.astype(jnp.bfloat16), "blk", scatter_dimension=1, tiled=True
        ).astype(jnp.float32),
    )
    grad_mod_low = to_low(grad_mod_part)
    grad_ada_w = left_product(conditioning, grad_mod_low)
    grad_ada_b = jnp.sum(grad_mod_low.astype(jnp.float32), axis=0)
    grad_caption = left_product(caption_rows, to_low(grad_memory_part))
    grad_ada_w, grad_ada_b, grad_caption = (
        lax.psum(grad_ada_w.astype(jnp.bfloat16), "seq").astype(jnp.float32),
        lax.psum(grad_ada_b.astype(jnp.bfloat16), "seq").astype(jnp.float32),
        lax.psum(grad_caption.astype(jnp.bfloat16), "seq").astype(jnp.float32),
    )
    shares = (
        lax.psum_scatter(grad_sin, ("seq", "blk"), scatter_dimension=0, tiled=True),
        lax.psum_scatter(grad_sout, ("seq", "blk"), scatter_dimension=0, tiled=True),
        lax.psum_scatter(grad_tin, ("seq", "blk"), scatter_dimension=0, tiled=True),
        lax.psum_scatter(grad_tout, ("seq", "blk"), scatter_dimension=0, tiled=True),
        lax.psum_scatter(grad_gain, ("seq", "blk"), scatter_dimension=0, tiled=True),
        lax.psum_scatter(grad_wquery, ("seq", "blk"), scatter_dimension=0, tiled=True),
        lax.psum_scatter(grad_cout, ("seq", "blk"), scatter_dimension=0, tiled=True),
        lax.psum_scatter(grad_hin, ("seq", "blk"), scatter_dimension=0, tiled=True),
        lax.psum_scatter(grad_hout, ("seq", "blk"), scatter_dimension=0, tiled=True),
    )
    (
        share_sin,
        share_sout,
        share_tin,
        share_tout,
        share_gain,
        share_query,
        share_cout,
        share_hin,
        share_hout,
    ) = shares
    return (
        to_low(result)[None],
        to_low(grad_input)[None],
        grad_ada_w,
        grad_ada_b,
        share_sin,
        share_sout,
        share_tin,
        share_tout,
        share_gain,
        share_query,
        grad_caption,
        share_cout,
        share_hin,
        share_hout,
    )


MESH = pl.DeviceIdType.MESH
BLOCKS = 18
LINES = 8
SHARD = 36
LINE = 4 * SHARD
WINDOW = 48
WIDE = LINES * LINE
MIB = 2**20


def place():
    seq = lax.axis_index("seq")
    blk = lax.axis_index("blk")
    x, c = seq // 2, seq % 2
    z, y = blk // 2, blk % 2
    x1, y1 = x + (1 - 2 * x) * (1 - c), y + (1 - 2 * y) * c
    x2, y2 = x + (1 - 2 * x) * c, y + (1 - 2 * y) * (1 - c)
    return x, c, y, z, x1, y1, x2, y2


def device(x, c, y, z):
    return {"seq": x * 2 + c, "blk": z * 2 + y}


def line_of(c, x, y):
    return (c * 2 + x) * 2 + y


def remote(src, dst, send_sem, recv_sem, where):
    return pltpu.make_async_remote_copy(
        src_ref=src,
        dst_ref=dst,
        send_sem=send_sem,
        recv_sem=recv_sem,
        device_id=where,
        device_id_type=MESH,
    )


def greet(others):
    barrier = pltpu.get_barrier_semaphore()
    for other in others:
        pl.semaphore_signal(barrier, inc=1, device_id=other, device_id_type=MESH)
    pl.semaphore_wait(barrier, len(others))


def left_at(t):
    at = jnp.minimum(t, 4)
    for first in (8, 9, 10, 11, 14, 15):
        at = at + jnp.where(t >= first, 1, 0)
    return at


def right_at(t):
    return jnp.where(t < 14, jnp.maximum(t - 3, 0), t - 13)


ROWS = 256
KEYS = 256
TEXT = 288
MOD = 9 * WIDE
MOD_TILES = 11
MOD_WIN = 128 * MOD_TILES
PARTS, HELD, LAST = 4, 4, 8
PAIR = 80
LEFT_SEM, SLOPE_SEM, SAVE_SEMS = 40, 42, 44
TILE = 384
SCALE = E ** (-0.5)


def nt(left, right):
    return lax.dot_general(
        left, right, (((1,), (1,)), ((), ())), preferred_element_type=jnp.float32
    )


def wide32(values):
    return values.astype(jnp.float32)


def loop(count, body):
    def step(index, carry):
        body(index)
        return carry

    lax.fori_loop(0, count, step, 0)


def each_rows(size, body, total=ROWS):
    loop(total // size, lambda i: body(pl.ds(pl.multiple_of(i * size, size), size)))


def each_cols(body):
    body(slice(0, 2 * TILE))
    body(slice(2 * TILE, 3 * TILE))


def identity(size):
    row = lax.broadcasted_iota(jnp.int32, (size, size), 0)
    col = lax.broadcasted_iota(jnp.int32, (size, size), 1)
    return to_low((row == col).astype(jnp.float32))


def transposed(same, values, to, start):
    for at in range(0, values.shape[1], TILE):
        to[start + at : start + at + TILE, :] = to_low(nt(same, values[:, at : at + TILE]))


def swap_rows():
    row = lax.broadcasted_iota(jnp.int32, (ROWS, ROWS), 0)
    col = lax.broadcasted_iota(jnp.int32, (ROWS, ROWS), 1)
    return to_low((((row & 15) << 4) + (row >> 4) == col).astype(jnp.float32))


def head_window(h):
    base = h * E
    start = jnp.minimum(base // 128, 7) * 128
    lane = lax.broadcasted_iota(jnp.int32, (1, 256), 1)
    on = (lane >= base - start) & (lane < base - start + E)
    return pl.ds(pl.multiple_of(start, 128), 256), on.astype(jnp.float32)


def soft(scores, bias, mask):
    scores = scores * SCALE
    if bias is not None:
        scores = scores + bias
    powers = jnp.exp(scores - jnp.max(scores, axis=-1, keepdims=True))
    probs = powers * (1.0 / jnp.sum(powers, axis=-1, keepdims=True))
    return probs if mask is None else probs * mask


def chains(h, groups):
    return [(window, rows, keys) for window in (head_window(h), head_window(h + H // 2)) for rows, keys in groups]


def split_rows(values, jobs):
    start = 0
    parts = []
    for _, rows, _ in jobs:
        size = rows.stop - rows.start
        parts.append(values[start : start + size])
        start += size
    return parts


def heads_forward(h, query, key, value, attn, groups, bias, mask):
    jobs = chains(h, groups)
    scores = [nt(query[rows, lanes] * to_low(on), key[keys, lanes]) for (lanes, on), rows, keys in jobs]
    probs = split_rows(to_low(soft(jnp.concatenate(scores), bias, mask)), jobs)
    parts = [linear(prob, value[keys, lanes]) * on for prob, ((lanes, on), rows, keys) in zip(probs, jobs)]
    for part, ((lanes, on), rows, keys) in zip(parts, jobs):
        attn[rows, lanes] = attn[rows, lanes] + to_low(part)


def text_heads_forward(h, query, key, value, attn, bias, mask):
    jobs = chains(h, VIDEOS)
    scores = [linear(query[rows, lanes] * to_low(on), key[lanes, keys]) for (lanes, on), rows, keys in jobs]
    probs = split_rows(to_low(soft(jnp.concatenate(scores), bias, mask)), jobs)
    parts = [nt(prob, value[lanes, keys]) * on for prob, ((lanes, on), rows, keys) in zip(probs, jobs)]
    for part, ((lanes, on), rows, keys) in zip(parts, jobs):
        attn[rows, lanes] = attn[rows, lanes] + to_low(part)


HALVES = [(slice(0, 128), slice(0, 128)), (slice(128, 256), slice(128, 256))]
VIDEOS = [(slice(0, 144), slice(0, 128)), (slice(112, 256), slice(128, 256))]


def regroup(back):
    row = lax.broadcasted_iota(jnp.int32, (ROWS, ROWS), 0)
    col = lax.broadcasted_iota(jnp.int32, (ROWS, ROWS), 1)
    if back:
        source = (((row >> 3) & 1) << 7) + ((row >> 4) << 3) + (row & 7)
    else:
        source = (((row >> 3) & 15) << 4) + ((row >> 7) << 3) + (row & 7)
    return to_low((source == col).astype(jnp.float32))


def temporal_bias(seg_in, seg_row):
    row = lax.broadcasted_iota(jnp.int32, (128, 128), 0)
    col = lax.broadcasted_iota(jnp.int32, (128, 128), 1)
    allowed = ((row & 7) == (col & 7)) & (seg_in[2, 0:128, 0:1] == seg_row[0:1, 0:128])
    return jnp.where(allowed, 0.0, MASKED)


def cross_bias():
    col = lax.broadcasted_iota(jnp.int32, (1, 128), 1)
    return jnp.where(col < L, 0.0, MASKED)


def cross_rows(seg_in):
    both = [1.0 - seg_in[0, 0:144, 0:1], seg_in[0, 112:256, 0:1]]
    return jnp.concatenate(both + both)


def move_lanes(to, value, from_start, to_start, width):
    left = min(from_start // 128 * 128, value.shape[1] - 256)
    right = min(to_start // 128 * 128, width - 256)
    off = to_start - right
    part = pltpu.roll(value[:, left : left + 256], (off - (from_start - left)) % 256, 1)
    lane = lax.broadcasted_iota(jnp.int32, part.shape, 1)
    lanes = slice(right, right + 256)
    to[:, lanes] = jnp.where((lane >= off) & (lane < off + SHARD), part, to[:, lanes])


def hidden_places():
    places = []
    for d in range(32):
        xp, cp, zp, yp = d // 16, d // 8 % 2, d // 2 % 4, d % 2
        for k in range(4):
            places.append((k, (4 * d + k) * SHARD, (((cp * 2 + xp) * 2 + yp) * 4 + zp) * SHARD))
    return places


def blk_peers(x, c, b):
    return [device(x, c, (b + k) % 2, ((b + k) % 8) // 2) for k in range(1, 8)]


def forward_kernel(
    spatial_in, spatial_out, temporal_in, temporal_out, cross_query, cross_out, hidden_in, hidden_out,
    tok, gain_one, cond, ada_bias, seg_in, seg_row, cot_i, turn_i, ada_i, caption_i, proj_i,
    wide, out, left_o, qkvs_o, qkvt_o, qc_o, mem_o, xhat_o, rstd_o, branch_o, slope_o, gfour_o, cot_o, mods_o, gate_o, gain_o,
    win, pair, far, lines, weights, tokp, cotp, tokf, xin, xp, left, qkvs, qkvt, qc, mem, text, mod, mods, xhat, rstd, branch, branchw, bias,
    stream, attnf, attnp, post, slope, gfour, gains, gain_at, gate,
    src, cot, turn, ada, caption, proj, mod_in, text_in, hidden,
    z_send, z_recv, l_send, l_recv, own_sem, w_sem, t_send, t_recv, a_send, a_recv, m_send, m_recv, x_send, x_recv,
    g_send, g_recv, save_sem, in_sem,
):
    x, c, y, z, x1, y1, x2, y2 = place()
    b = z * 2 + y
    near = [device(x, c, y, (z + k) % 4) for k in (1, 2, 3)]
    beside, across = device(x, c, y, z + 1 - 2 * (z % 2)), device(x, c, y, 3 - z)
    middle = (z == 1) | (z == 2)
    first, second, twin = device(x1, c, y1, z), device(x2, c, y2, z), device(x, 1 - c, y, z)
    peers = blk_peers(x, c, b)
    greet(peers + [device(1 - x, c, y, z), twin])
    mine, line3 = line_of(c, x, y), line_of(c, 1 - x, 1 - y)

    def hops(t, core):
        turn_round = core + (1 - core) * (t % 4 == 2)
        xa, ya = x + (1 - 2 * x) * (1 - turn_round), y + (1 - 2 * y) * turn_round
        xb, yb = x + (1 - 2 * x) * turn_round, y + (1 - 2 * y) * (1 - turn_round)
        return (xa, ya), (xb, yb)

    def z_one(t):
        return remote(src.at[t], win.at[t % PARTS], z_send.at[t, 0], z_recv.at[t, 0], beside)

    def z_two(t):
        return remote(pair.at[t % PARTS], far.at[t % PARTS], z_send.at[t, 1], z_recv.at[t, 1], across)

    def z_three(t):
        return remote(far.at[t % PARTS], far.at[t % PARTS], z_send.at[t, 2], z_recv.at[t, 2], beside)

    def wide_line(t, line):
        return wide.at[t, pl.ds(pl.multiple_of(line * LINE, 16), LINE)]

    def own(t):
        return pltpu.make_async_copy(lines.at[t % HELD], wide_line(t, mine), own_sem.at[t])

    def line_copy(t, to, line, index, where):
        return remote(to, wide_line(t, line), l_send.at[t, index], l_recv.at[t, index], where)

    def sends(t, index):
        (xa, ya), (xb, yb) = hops(t, c)
        one, two = device(xa, c, ya, z), device(xb, c, yb, z)
        line1, line2 = line_of(c, xa, ya), line_of(c, xb, yb)
        line, where = (
            (mine, one), (mine, two), (mine, twin), (line1, two),
            (line1, twin), (line2, twin), (line3, twin),
        )[index]
        from_here = lines.at[t % HELD] if index < 3 else wide_line(t, line)
        return line_copy(t, from_here, line, index, where)

    def arrives(t, line, index):
        line_copy(t, wide_line(t, line), line, index, first).wait_recv()

    def tick(t):
        @pl.when((t >= 4) & (t < BLOCKS + 4))
        def _():
            now = t - 4

            @pl.when(middle)
            def _():
                z_two(now).wait_send()
                z_three(now).wait_send()

            @pl.when(jnp.logical_not(middle))
            def _():
                z_three(now).wait_recv()

            @pl.when(now >= HELD)
            def _():
                for index in range(3):
                    sends(now - HELD, index).wait_send()
                own(now - HELD).wait()

            def line_from(low, high):
                at = now % HELD
                lines[at, 0:64] = low[0:64]
                lines[at, 64:80] = low[64:80] + high[0:16]
                lines[at, 80:144] = high[16:80]

            @pl.when(z < 2)
            def _():
                line_from(pair[now % PARTS], far[now % PARTS])

            @pl.when(z >= 2)
            def _():
                line_from(far[now % PARTS], pair[now % PARTS])

            for index in range(3):
                sends(now, index).start()
            own(now).start()

        @pl.when((t >= 2) & (t < BLOCKS + 2) & middle)
        def _():
            z_two(t - 2).wait_recv()
            z_three(t - 2).start()

        @pl.when((t >= 1) & (t < BLOCKS + 1))
        def _():
            now = t - 1
            z_one(now).wait_recv()

            def pair_from(even, odd):
                at = now % PARTS
                pair[at, 0:32] = even[0:32]
                pair[at, 32:48] = even[32:48] + odd[0:16]
                pair[at, 48:80] = odd[16:48]

            @pl.when(z % 2 == 0)
            def _():
                pair_from(src[now], win[now % PARTS])

            @pl.when(z % 2 == 1)
            def _():
                pair_from(win[now % PARTS], src[now])

            @pl.when(middle)
            def _():
                z_two(now).start()

        @pl.when(t < BLOCKS)
        def _():
            z_one(t).start()

        @pl.when((t >= 6) & (t < BLOCKS + 6))
        def _():
            now = t - 6
            xa, ya = hops(now, c)[0]
            arrives(now, line_of(c, xa, ya), 0)
            for index in (3, 4):
                sends(now, index).start()

        @pl.when(t >= LAST)
        def _():
            now = t - LAST
            xb, yb = hops(now, c)[1]
            arrives(now, line_of(c, xb, yb), 1)
            sends(now, 5).start()
            arrives(now, line3, 3)
            sends(now, 6).start()

    done = [0]

    def pump(until):
        until = min(until, BLOCKS + LAST)
        if until > done[0]:
            start = done[0]
            loop(until - start, lambda i: tick(i + start))
            done[0] = until

    def poke():
        pump(done[0] + 1)

    def weight_copy(block):
        return pltpu.make_async_copy(wide.at[block], weights.at[block % 2], w_sem.at[block % 2])

    loaded = set()

    def begin(block):
        if block in loaded:
            return
        loaded.add(block)
        pump(block + LAST + 1)
        near_at, far_at = hops(block, 1 - c)
        places = [(x, y), near_at, far_at, (1 - x, 1 - y)]
        for (xl, yl), index in zip(places, (2, 4, 5, 6)):
            arrives(block, line_of(1 - c, xl, yl), index)
        if block >= BLOCKS - HELD:
            own(block).wait()
        weight_copy(block).start()

    def load(block):
        begin(block)
        weight_copy(block).wait()
        if 3 <= block < BLOCKS - 1:
            begin(block + 1)

    def times(values, block, emit):
        def tile(cols):
            emit(cols, linear(values[...], weights[block % 2, :, cols]))

        each_cols(tile)

    saves = []
    held = {}

    def save(from_ref, to_ref, name=None):
        if name is None:
            name = len(saves)
            saves.append(name)
        held[name] = pltpu.make_async_copy(from_ref, to_ref, save_sem.at[name])
        held[name].start()

    def settle(name):
        if name in held:
            held.pop(name).wait()

    def turned(values, index):
        slot = index % 2
        settle(LEFT_SEM + slot)

        def tile(cols):
            low = to_low(nt(values[...], turn[cols, :]))
            xp[:, cols] = low
            transposed(identity(TILE), low, left.at[slot], cols.start)

        each_cols(tile)
        save(left.at[slot], left_o.at[index], LEFT_SEM + slot)

    fetches = [
        pltpu.make_async_copy(from_ref, to_ref, in_sem.at[at])
        for at, (from_ref, to_ref) in enumerate(
            ((ada_i, ada), (turn_i, turn), (cot_i, cot), (caption_i, caption), (proj_i, proj))
        )
    ]
    for copy in fetches:
        copy.start()

    def shift(rows, first):
        row = lax.broadcasted_iota(jnp.int32, (WINDOW, rows), 0) - 4 * z
        col = lax.broadcasted_iota(jnp.int32, (WINDOW, rows), 1)
        return to_low(((row >= 0) & (row < SHARD) & (row + first == col)).astype(jnp.float32))

    def window(at, values):
        src[at] = to_low(linear(shift(SHARD, 0), values))

    for j in range(3):
        window(j, spatial_in[:, WIDE * j : WIDE * j + WIDE])
    pump(2)
    window(3, spatial_out[...])
    for j in range(3):
        window(4 + j, temporal_in[:, WIDE * j : WIDE * j + WIDE])
    window(7, temporal_out[...])
    window(8, cross_query[...])
    window(9, cross_out[...])
    pump(4)

    def m_copy(k, at):
        return remote(mod_in, mod.at[at], m_send.at[k - 1], m_recv.at[k - 1], peers[k - 1])

    fetches[0].wait()
    part = wide32(to_low(nt(cond[...], ada[...]) + wide32(ada_bias[...])))[0:8]
    part = jnp.concatenate([part, jnp.zeros((8, MOD_WIN - MOD // 8), jnp.float32)], axis=1)
    part = pltpu.roll(part, 16 * b, 1)
    tiles = [part[row : row + 1, 128 * tile : 128 * tile + 128] for row in range(2) for tile in range(MOD_TILES)]
    mod_in[...] = to_low(jnp.concatenate(tiles + [jnp.zeros((32 - 2 * MOD_TILES, 128), jnp.float32)]))
    for k in range(1, 8):
        m_copy(k, b).start()
    mod[b] = mod_in[...]
    swap = swap_rows()
    tokp[...] = to_low(linear(swap, tok[...]))

    def t_copy(k):
        to = (b + k) % 8
        part = tokp.at[pl.ds(pl.multiple_of(32 * to, 32), 32)]
        return remote(part, tokf.at[b], t_send.at[k - 1], t_recv.at[k - 1], peers[k - 1])

    def t_wait(k):
        of = (b + 8 - k) % 8
        remote(tokp.at[pl.ds(0, 32)], tokf.at[of], t_send.at[k - 1], t_recv.at[k - 1], peers[k - 1]).wait_recv()

    pump(5)
    for k in range(1, 8):
        t_copy(k).start()
    tokf[b] = tokp[pl.ds(pl.multiple_of(32 * b, 32), 32)]

    def g_copy(at, from_at, to):
        return remote(gains.at[from_at], gain_at.at[at], g_send.at[at], g_recv.at[at], to)

    spread = jnp.concatenate([wide32(gain_one[...]), jnp.zeros((8, WIDE - SHARD), jnp.float32)], axis=1)
    gains[0] = pltpu.roll(spread, SHARD * ((x * 2 + c) * 8 + b), 1)
    g_copy(0, 0, twin).start()
    pump(6)
    fetches[2].wait()
    cotp[...] = to_low(linear(swap, cot[...]))
    save(cotp, cot_o)

    def x_copy(k, at):
        return remote(text_in, text.at[at, y], x_send.at[k - 1], x_recv.at[k - 1], near[k - 1])

    def x_over(at):
        return remote(text.at[:, at], text.at[:, at], x_send.at[3], x_recv.at[3], device(x, c, 1 - y, z))

    for k in range(1, 8):
        m_copy(k, (b + 8 - k) % 8).wait_recv()
    mods[...] = jnp.zeros_like(mods)
    for k in range(8):
        part = wide32(mod[k])
        for row in range(2):
            for tile in range(MOD_TILES):
                lanes = slice(1280 * k + 128 * tile, 1280 * k + 128 * tile + 128)
                at = row * MOD_TILES + tile
                mods[row : row + 1, lanes] = mods[row : row + 1, lanes] + part[at : at + 1]
    save(mods, mods_o)
    g_copy(0, 0, twin).wait_recv()
    gains[1] = gains[0] + gain_at[0]
    g_copy(1, 1, first).start()
    pump(7)
    fetches[3].wait()
    fetches[4].wait()
    text_in[...] = jnp.zeros_like(text_in)
    for v in range(2):
        text_in[:, 128 * v : 128 * v + L] = to_low(nt(proj[...], caption[v]))
    for k in (1, 2, 3):
        x_copy(k, z).start()
    text[z, y] = text_in[...]
    pump(8)
    hidden[...] = jnp.zeros_like(hidden)
    for k, natural, placed in hidden_places():
        start = natural // WIDE * WIDE
        move_lanes(hidden.at[k], wide32(hidden_in[:, start : start + WIDE]), natural - start, placed, WIDE)
    for k in range(4):
        window(10 + 2 * k, to_low(hidden[k]))
        src[11 + 2 * k] = to_low(linear(shift(4 * SHARD, SHARD * k), hidden_out[...]))
    fetches[1].wait()

    def pick(piece, seg):
        lanes = slice(WIDE * piece, WIDE * piece + WIDE)
        return jnp.where(seg > 0.5, mods[1:2, lanes], mods[0:1, lanes])

    def normal(values, rows, index):
        center = values - jnp.mean(values, axis=-1, keepdims=True)
        factor = lax.rsqrt(jnp.mean(center * center, axis=-1, keepdims=True) + EPSILON)
        scaled = center * factor
        xhat[index, rows, :] = to_low(scaled)
        rstd[index, rows, :] = jnp.broadcast_to(factor, (factor.shape[0], 128))
        return scaled

    for k in range(1, 8):
        t_wait(k)
    g_copy(1, 1, first).wait_recv()
    gains[2] = gains[1] + gain_at[1]
    g_copy(2, 2, second).start()

    def spatial_rows(i):
        seg = jnp.concatenate([seg_in[1, 0:16, 0:1], seg_in[1, 128:144, 0:1]])
        values = wide32(tokf[i])
        center = values - jnp.mean(values, axis=-1, keepdims=True)
        factor = lax.rsqrt(jnp.mean(center * center, axis=-1, keepdims=True) + EPSILON)
        scaled = center * factor
        ready = to_low(scaled * (1.0 + pick(1, seg)) + pick(0, seg))
        low = to_low(scaled)
        spread = jnp.broadcast_to(factor, (32, 128))
        for f in range(2):
            rows = pl.ds(pl.multiple_of(128 * f + 16 * i, 16), 16)
            part = slice(16 * f, 16 * f + 16)
            xhat[0, rows, :] = low[part]
            rstd[0, rows, :] = spread[part]
            xin[rows, :] = ready[part]

    loop(8, spatial_rows)
    save(xhat.at[0], xhat_o.at[0])
    save(rstd.at[0], rstd_o.at[0])
    turned(xin, 10)
    for j in range(3):
        load(j)

        def emit(cols, value, j=j):
            qkvs[j, :, cols] = to_low(value)

        times(xp, j, emit)
    save(qkvs, qkvs_o)
    g_copy(2, 2, second).wait_recv()
    gains[3] = gains[2] + gain_at[2]
    for k in (1, 2, 3):
        remote(gains.at[3], gain_at.at[2 + k], g_send.at[2 + k], g_recv.at[2 + k], near[k - 1]).start()
    for k in (1, 2, 3):
        x_copy(k, (z + 4 - k) % 4).wait_recv()
    x_over(y).start()
    attnf[...] = jnp.zeros_like(attnf)

    def spatial_heads(h):
        heads_forward(h, qkvs.at[0], qkvs.at[1], qkvs.at[2], attnf, HALVES, None, None)

    loop(4, spatial_heads)
    poke()
    loop(4, lambda h: spatial_heads(h + 4))
    for k in (1, 2, 3):
        remote(gains.at[3], gain_at.at[2 + k], g_send.at[2 + k], g_recv.at[2 + k], near[k - 1]).wait_recv()
    gains[0 + 4] = gains[3] + gain_at[3] + gain_at[4] + gain_at[5]
    save(gains.at[4], gain_o)

    def a_copy(k, f):
        to = (b + k) % 8
        part = attnf.at[pl.ds(pl.multiple_of(128 * f + 16 * to, 16), 16)]
        return remote(part, attnp.at[2 * b + f], a_send.at[k - 1, f], a_recv.at[k - 1, f], peers[k - 1])

    def a_wait(k, f):
        of = (b + 8 - k) % 8
        part = attnf.at[pl.ds(0, 16)]
        remote(part, attnp.at[2 * of + f], a_send.at[k - 1, f], a_recv.at[k - 1, f], peers[k - 1]).wait_recv()

    for k in range(1, 8):
        for f in range(2):
            a_copy(k, f).start()
    for f in range(2):
        attnp[2 * b + f] = attnf[pl.ds(pl.multiple_of(128 * f + 16 * b, 16), 16)]
    pump(done[0] + 2)
    for k in range(1, 8):
        for f in range(2):
            a_wait(k, f)
    xin[...] = attnp[...].reshape(ROWS, WIDE)
    turned(xin, 9)
    load(3)

    def emit_branch(cols, value):
        branchw[:, cols] = value

    times(xp, 3, emit_branch)

    def after_spatial(rows):
        seg = seg_in[0, rows, 0:1]
        value = branchw[rows, :]
        branch[0, rows, :] = to_low(value)
        value = wide32(tokp[rows, :]) + pick(2, seg) * value
        stream[rows, :] = value
        xin[rows, :] = to_low(normal(value, rows, 1) * (1.0 + pick(4, seg)) + pick(3, seg))

    each_rows(32, after_spatial)
    save(branch.at[0], branch_o.at[0])
    save(xhat.at[1], xhat_o.at[1])
    save(rstd.at[1], rstd_o.at[1])

    for k in range(1, 8):
        for f in range(2):
            a_copy(k, f).wait_send()
    attnf[...] = to_low(linear(regroup(False), xin[...]))
    turned(attnf, 8)
    for j in range(3):
        load(4 + j)

        def emit(cols, value, j=j):
            qkvt[j, :, cols] = to_low(value)

        times(xp, 4 + j, emit)
    save(qkvt, qkvt_o)
    attnf[...] = jnp.zeros_like(attnf)

    bias[...] = temporal_bias(seg_in, seg_row)

    def temporal_heads(h):
        heads_forward(
            h, qkvt.at[0], qkvt.at[1], qkvt.at[2], attnf, HALVES, jnp.concatenate([bias[...]] * 4), None
        )

    loop(4, temporal_heads)
    poke()
    loop(4, lambda h: temporal_heads(h + 4))
    xin[...] = to_low(linear(regroup(True), attnf[...]))
    turned(xin, 7)
    load(7)
    times(xp, 7, emit_branch)

    def after_temporal(rows):
        seg = seg_in[0, rows, 0:1]
        value = branchw[rows, :]
        branch[1, rows, :] = to_low(value)
        value = stream[rows, :] + pick(5, seg) * value
        stream[rows, :] = value
        xin[rows, :] = to_low(normal(value, rows, 2) * gains[4, 0:1, :])

    each_rows(32, after_temporal)
    save(branch.at[1], branch_o.at[1])
    save(xhat.at[2], xhat_o.at[2])
    save(rstd.at[2], rstd_o.at[2])

    turned(xin, 6)
    load(8)

    def emit_query(cols, value):
        qc[:, cols] = to_low(value)

    times(xp, 8, emit_query)
    save(qc, qc_o)
    x_over(1 - y).wait_recv()
    for k in range(8):
        mem[k // 4, TEXT * (k % 4) : TEXT * (k % 4) + TEXT, :] = text[k // 2, k % 2]
    save(mem, mem_o)
    attnf[...] = jnp.zeros_like(attnf)

    def cross_heads(h):
        text_heads_forward(h, qc, mem.at[0], mem.at[1], attnf, cross_bias(), cross_rows(seg_in))

    loop(4, cross_heads)
    poke()
    loop(4, lambda h: cross_heads(h + 4))
    xin[...] = attnf[...]
    turned(xin, 5)
    load(9)
    times(xp, 9, emit_branch)

    def after_cross(rows):
        seg = seg_in[0, rows, 0:1]
        value = stream[rows, :] + branchw[rows, :]
        stream[rows, :] = value
        xin[rows, :] = to_low(normal(value, rows, 3) * (1.0 + pick(7, seg)) + pick(6, seg))
        gfour[rows, :] = to_low(wide32(cotp[rows, :]) * pick(8, seg))

    each_rows(32, after_cross)
    save(xhat.at[3], xhat_o.at[3])
    save(rstd.at[3], rstd_o.at[3])
    save(gfour, gfour_o)

    turned(xin, 4)
    for k in range(4):
        slot = k % 2
        load(10 + 2 * k)
        settle(SLOPE_SEM + slot)
        settle(LEFT_SEM + slot)

        def emit_hidden(cols, value, slot=slot):
            inner = math.sqrt(2.0 / math.pi) * (value + 0.044715 * value * value * value)
            bent = jnp.tanh(inner)
            half = 0.5 * (1.0 + bent)
            tilt = math.sqrt(2.0 / math.pi) * (1.0 + 3 * 0.044715 * value * value)
            slope[slot, :, cols] = to_low(half + 0.5 * value * (1.0 - bent * bent) * tilt)
            low = to_low(value * half)
            post[:, cols] = low
            transposed(identity(TILE), low, left.at[slot], cols.start)

        times(xp, 10 + 2 * k, emit_hidden)
        save(slope.at[slot], slope_o.at[k], SLOPE_SEM + slot)
        save(left.at[slot], left_o.at[k], LEFT_SEM + slot)
        load(11 + 2 * k)

        def emit_out(cols, value, k=k):
            branchw[:, cols] = value if k == 0 else branchw[:, cols] + value

        times(post, 11 + 2 * k, emit_out)

    gate[...] = jnp.zeros_like(gate)

    def last(rows):
        seg = seg_in[0, rows, 0:1]
        value = branchw[rows, :]
        xin[rows, :] = to_low(stream[rows, :] + pick(8, seg) * value)
        value = wide32(cotp[rows, :]) * value
        later = jnp.sum(value * seg, axis=0, keepdims=True)
        every = jnp.sum(value, axis=0, keepdims=True)
        gate[0:1, :] = gate[0:1, :] + (every - later)
        gate[1:2, :] = gate[1:2, :] + later

    each_rows(32, last)
    save(gate, gate_o)
    out[...] = to_low(linear(swap_rows(), xin[...]))

    for copy in held.values():
        copy.wait()
    for k in range(1, 8):
        t_copy(k).wait_send()
        m_copy(k, b).wait_send()
    for k in (1, 2, 3):
        x_copy(k, z).wait_send()
    x_over(y).wait_send()
    for at, to in ((0, twin), (1, first), (2, second)):
        g_copy(at, at, to).wait_send()
    for k in (1, 2, 3):
        remote(gains.at[3], gain_at.at[2 + k], g_send.at[2 + k], g_recv.at[2 + k], near[k - 1]).wait_send()

    for t in range(BLOCKS - HELD, BLOCKS):
        for index in range(3):
            sends(t, index).wait_send()

    def finish(t):
        z_one(t).wait_send()
        for index in range(3, 7):
            sends(t, index).wait_send()

    loop(BLOCKS, finish)


ANY = pl.BlockSpec(memory_space=pl.ANY)
IN_VMEM = pl.BlockSpec(memory_space=pltpu.VMEM)


def forward(*operands):
    low, full = jnp.bfloat16, jnp.float32
    dma = pltpu.SemaphoreType.DMA
    hbm = [
        ((BLOCKS, WIDE, WIDE), low),
        ((ROWS, WIDE), low),
        ((11, WIDE, ROWS), low),
        ((3, ROWS, WIDE), low),
        ((3, ROWS, WIDE), low),
        ((ROWS, WIDE), low),
        ((2, WIDE, KEYS), low),
        ((4, ROWS, WIDE), low),
        ((4, ROWS, 128), full),
        ((2, ROWS, WIDE), low),
        ((4, ROWS, WIDE), low),
        ((ROWS, WIDE), low),
        ((ROWS, WIDE), low),
        ((8, MOD), full),
        ((8, WIDE), full),
        ((8, WIDE), full),
    ]
    vmem = [
        ((PARTS, WINDOW, WIDE), low),
        ((PARTS, PAIR, WIDE), low),
        ((PARTS, PAIR, WIDE), low),
        ((HELD, LINE, WIDE), low),
        ((2, WIDE, WIDE), low),
        ((ROWS, WIDE), low),
        ((ROWS, WIDE), low),
        ((8, 32, WIDE), low),
        ((ROWS, WIDE), low),
        ((ROWS, WIDE), low),
        ((2, WIDE, ROWS), low),
        ((3, ROWS, WIDE), low),
        ((3, ROWS, WIDE), low),
        ((ROWS, WIDE), low),
        ((2, WIDE, KEYS), low),
        ((4, 2, TEXT, KEYS), low),
        ((8, 32, 128), low),
        ((8, MOD), full),
        ((4, ROWS, WIDE), low),
        ((4, ROWS, 128), full),
        ((2, ROWS, WIDE), low),
        ((ROWS, WIDE), full),
        ((128, 128), full),
        ((ROWS, WIDE), full),
        ((ROWS, WIDE), low),
        ((16, 16, WIDE), low),
        ((ROWS, WIDE), low),
        ((2, ROWS, WIDE), low),
        ((ROWS, WIDE), low),
        ((5, 8, WIDE), full),
        ((6, 8, WIDE), full),
        ((8, WIDE), full),
        ((BLOCKS, WINDOW, WIDE), low),
        ((ROWS, WIDE), low),
        ((WIDE, WIDE), low),
        ((MOD // 8, WIDE), low),
        ((2, L, 4096), low),
        ((TEXT, 4096), low),
        ((32, 128), low),
        ((TEXT, KEYS), low),
        ((4, SHARD, WIDE), full),
    ]
    return pl.pallas_call(
        forward_kernel,
        out_shape=[jax.ShapeDtypeStruct(*shape) for shape in hbm],
        in_specs=[IN_VMEM] * 14 + [ANY] * 5,
        out_specs=[ANY, IN_VMEM] + [ANY] * 14,
        scratch_shapes=[pltpu.VMEM(*shape) for shape in vmem]
        + [
            dma((BLOCKS, 3)), dma((BLOCKS, 3)), dma((BLOCKS, 7)), dma((BLOCKS, 7)), dma((BLOCKS,)), dma((2,)),
            dma((7,)), dma((7,)), dma((7, 2)), dma((7, 2)), dma((7,)), dma((7,)), dma((4,)), dma((4,)),
            dma((6,)), dma((6,)), dma((SAVE_SEMS,)), dma((5,)),
        ],
        compiler_params=pltpu.CompilerParams(
            collective_id=0, has_side_effects=True, vmem_limit_bytes=60 * MIB
        ),
        name="forward",
    )(*operands)


def tn(left, right):
    return lax.dot_general(
        left, right, (((0,), (0,)), ((), ())), preferred_element_type=jnp.float32
    )


def text_heads_backward(h, query, key, value, grad, dquery, dkey, dvalue, bias, mask):
    jobs = chains(h, VIDEOS)
    scores, grads = [], []
    for (lanes, on), rows, keys in jobs:
        low_on = to_low(on)
        scores.append(linear(query[rows, lanes] * low_on, key[lanes, keys]))
        grads.append(linear(grad[rows, lanes] * low_on, value[lanes, keys]))
    probs = soft(jnp.concatenate(scores), bias, mask)
    grad_probs = jnp.concatenate(grads)
    delta = jnp.sum(grad_probs * probs, axis=-1, keepdims=True)
    slopes = split_rows(to_low(probs * (grad_probs - delta)), jobs)
    probs = split_rows(to_low(probs), jobs)
    parts = []
    for slope, prob, ((lanes, on), rows, keys) in zip(slopes, probs, jobs):
        low_on = to_low(on)
        parts.append(
            (
                to_low(nt(slope, key[lanes, keys]) * (on * SCALE)),
                to_low(tn(query[rows, lanes] * low_on, slope) * SCALE),
                to_low(tn(grad[rows, lanes] * low_on, prob)),
            )
        )
    for (by_query, by_key, by_value), ((lanes, on), rows, keys) in zip(parts, jobs):
        dquery[rows, lanes] = dquery[rows, lanes] + by_query
        dkey[lanes, keys] = dkey[lanes, keys] + by_key
        dvalue[lanes, keys] = dvalue[lanes, keys] + by_value


def heads_backward(h, query, key, value, grad, dquery, dkey, dvalue, groups, bias, mask):
    jobs = chains(h, groups)
    scores, grads = [], []
    for (lanes, on), rows, keys in jobs:
        low_on = to_low(on)
        scores.append(nt(query[rows, lanes] * low_on, key[keys, lanes]))
        grads.append(nt(grad[rows, lanes] * low_on, value[keys, lanes]))
    probs = soft(jnp.concatenate(scores), bias, mask)
    grad_probs = jnp.concatenate(grads)
    delta = jnp.sum(grad_probs * probs, axis=-1, keepdims=True)
    slopes = split_rows(to_low(probs * (grad_probs - delta)), jobs)
    probs = split_rows(to_low(probs), jobs)
    parts = []
    for slope, prob, ((lanes, on), rows, keys) in zip(slopes, probs, jobs):
        parts.append(
            (
                to_low(linear(slope, key[keys, lanes]) * (on * SCALE)),
                to_low(tn(slope, query[rows, lanes]) * (on * SCALE)),
                to_low(tn(prob, grad[rows, lanes]) * on),
            )
        )
    for (by_query, by_key, by_value), ((lanes, on), rows, keys) in zip(parts, jobs):
        dquery[rows, lanes] = dquery[rows, lanes] + by_query
        dkey[keys, lanes] = dkey[keys, lanes] + by_key
        dvalue[keys, lanes] = dvalue[keys, lanes] + by_value


def backward_kernel(
    wide, left_i, qkvs_i, qkvt_i, qc_i, mem_i, xhat_i, rstd_i, branch_i, slope_i, gfour_i, cot_i, mods_i, gate_i, gain_i,
    caption_i, seg_in, seg_row, turn, cond_in,
    total, gtok, gain_o, caption_o, mod_o,
    weights, left, right, qkv, xhat, rstd, branch, slope, mods, gain, bias, stream, work, grad, xin, gm, mem, dmem, text, text_at, text_sum, cap, cap_out, cap_in, cap_own, cap_at, mod_out, mod,
    seqs, gains, gain_at, gframe, back,
    s0, r0, s1, r1, s2, r2, k2, s3, pass_in, pass_out, far_in, close, close_in, share,
    in_sem, w_sem, s0_sem, r0_sem, s1_sem, r1_sem, s2_sem, r2_sem, z_send, z_recv, share_sem,
    a_send, a_recv, u_send, u_recv, x_send, x_recv, m_send, m_recv, q_send, q_recv, g_send, g_recv,
    cap_sem, c_send, c_recv, left_sem,
):
    x, c, y, z, x1, y1, x2, y2 = place()
    b = z * 2 + y
    near = [device(x, c, y, (z + k) % 4) for k in (1, 2, 3)]
    first, second, twin = device(x1, c, y1, z), device(x2, c, y2, z), device(x, 1 - c, y, z)
    peers = blk_peers(x, c, b)
    across = [twin, device(1 - x, c, y, z), device(1 - x, 1 - c, y, z)]
    greet(peers + across)

    fetches = {}

    def fetch(name, from_ref, to_ref):
        fetches[name] = pltpu.make_async_copy(from_ref, to_ref, in_sem.at[name])
        fetches[name].start()

    def have(name):
        if name in fetches:
            fetches.pop(name).wait()

    fetch(0, gfour_i, right.at[0])
    for k in range(4):
        fetch(1 + k, left_i.at[k], left.at[k])
    fetch(12, mods_i, mods)
    fetch(13, gain_i, gain)
    fetch(14, slope_i.at[0], slope.at[0])
    fetch(15, slope_i.at[1], slope.at[1])
    fetch(16, xhat_i.at[3], xhat.at[1])
    fetch(17, rstd_i.at[3], rstd.at[1])
    fetch(18, cot_i, xin)
    fetch(19, gate_i, work.at[0:8])

    def weight(block):
        slot = WEIGHT_ORDER.index(block) % 2
        return weights.at[slot]

    def prefetch(at):
        if at < len(WEIGHT_ORDER):
            copy = pltpu.make_async_copy(wide.at[WEIGHT_ORDER[at]], weights.at[at % 2], w_sem.at[at % 2])
            copy.start()
            fetches["w", WEIGHT_ORDER[at]] = copy

    def release(block):
        prefetch(WEIGHT_ORDER.index(block) + 2)

    prefetch(0)
    prefetch(1)

    away = [(1 - x) * 2 + 1 - y, x2 * 2 + y2]
    stay = [x1 * 2 + y1, x * 2 + y]

    def product(t, core, xl):
        rows = pl.ds(pl.multiple_of(line_of(core, xl, 0) * LINE, 16), 2 * LINE)
        return linear(left[left_at(t) % 4, rows, :], right[right_at(t)])

    def left_copy(t):
        return pltpu.make_async_copy(left_i.at[left_at(t)], left.at[left_at(t) % 4], left_sem.at[0])

    def left_next(t):
        return (t >= 4) & (t < BLOCKS) & (left_at(t) != left_at(t - 1))

    def copy0(t, l):
        pair = pl.ds(2 * l, 2)
        return remote(s0.at[t % 2, pair], r0.at[t % 4, pair], s0_sem.at[t % 2, l], r0_sem.at[t % 4, l], twin)

    def copy1(t, l):
        return remote(s1.at[t % 2, away[l]], r1.at[t % 4, l], s1_sem.at[t % 2, l], r1_sem.at[t % 4, l], second)

    def copy2(t):
        return remote(s2.at[t % 2], r2.at[t % 4], s2_sem.at[t % 2], r2_sem.at[t % 4], first)

    beside, opposite = device(x, c, y, z + 1 - 2 * (z % 2)), device(x, c, y, 3 - z)
    middle = (z == 1) | (z == 2)
    near_rows = pl.ds(pl.multiple_of(64 * (z // 2), 16), PAIR)
    far_rows = pl.ds(pl.multiple_of(64 - 64 * (z // 2), 16), PAIR)
    own_rows = pl.ds(pl.multiple_of(32 * (z % 2), 16), WINDOW)
    beside_rows = pl.ds(pl.multiple_of(32 - 32 * (z % 2), 16), WINDOW)

    def z_one(t):
        return remote(s3.at[t % 4, far_rows], pass_in.at[t % 4], z_send.at[0, t % 4], z_recv.at[0, t % 4], beside)

    def z_two(t):
        return remote(pass_out.at[t % 2], far_in.at[t % 4], z_send.at[1, t % 4], z_recv.at[1, t % 4], opposite)

    def z_three(t):
        return remote(
            close.at[t % 2, beside_rows], close_in.at[t % 4], z_send.at[2, t % 4], z_recv.at[2, t % 4], beside
        )

    def share_copy(t):
        return pltpu.make_async_copy(share.at[t % 2], total.at[t], share_sem.at[t % 2])

    def tick(t):
        @pl.when(t >= 10)
        def _():
            now = t - 10
            z_three(now).wait_recv()
            value = wide32(close[now % 2, own_rows]) + wide32(close_in[now % 4])

            @pl.when(jnp.logical_not(middle))
            def _():
                z_one(now).wait_send()

            @pl.when(now >= 2)
            def _():
                share_copy(now - 2).wait()
            share[now % 2] = value
            share_copy(now).start()

        @pl.when((t >= 8) & (t < BLOCKS + 8))
        def _():
            now = t - 8

            @pl.when(now >= 2)
            def _():
                z_three(now - 2).wait_send()

            @pl.when(middle)
            def _():
                z_two(now).wait_recv()
                close[now % 2] = to_low(wide32(s3[now % 4, near_rows]) + wide32(far_in[now % 4]))

            @pl.when(jnp.logical_not(middle))
            def _():
                close[now % 2] = s3[now % 4, near_rows]

            z_three(now).start()

        @pl.when((t >= 7) & (t < BLOCKS + 7) & middle)
        def _():
            now = t - 7
            z_one(now).wait_recv()

            @pl.when(now >= 2)
            def _():
                z_two(now - 2).wait_send()
            pass_out[now % 2] = to_low(wide32(s3[now % 4, far_rows]) + wide32(pass_in[now % 4]))
            z_two(now).start()

        @pl.when((t >= 6) & (t < BLOCKS + 6))
        def _():
            now = t - 6
            copy2(now).wait_recv()
            s3[now % 4] = to_low(k2[now % 2] + wide32(r2[now % 4]))

            @pl.when(jnp.logical_not(middle))
            def _():
                z_one(now).start()

        @pl.when((t >= 4) & (t < BLOCKS + 4))
        def _():
            now = t - 4
            copy1(now, 0).wait_recv()

            @pl.when(now >= 2)
            def _():
                copy2(now - 2).wait_send()
            s2[now % 2] = to_low(wide32(s1[now % 2, stay[0]]) + wide32(r1[now % 4, 0]))
            copy2(now).start()
            copy1(now, 1).wait_recv()
            k2[now % 2] = wide32(s1[now % 2, stay[1]]) + wide32(r1[now % 4, 1])

        @pl.when((t >= 2) & (t < BLOCKS + 2))
        def _():
            now = t - 2

            @pl.when(now >= 2)
            def _():
                for l in range(2):
                    copy1(now - 2, l).wait_send()
            for l in range(2):
                copy0(now, l).wait_recv()
                value = product(now, c, l)
                for part in range(2):
                    line = 2 * l + part
                    summed = value[part * LINE : part * LINE + LINE] + wide32(r0[now % 4, line])
                    s1[now % 2, line] = to_low(summed)
            for l in range(2):
                copy1(now, l).start()

        @pl.when(left_next(t))
        def _():
            left_copy(t).wait()

        @pl.when(t < BLOCKS)
        def _():
            for l in range(2):
                @pl.when(t >= 2)
                def _():
                    copy0(t - 2, l).wait_send()
                value = to_low(product(t, 1 - c, l))
                s0[t % 2, 2 * l] = value[:LINE]
                s0[t % 2, 2 * l + 1] = value[LINE:]
                copy0(t, l).start()

        @pl.when(left_next(t + 1))
        def _():
            left_copy(t + 1).start()

    done = [0]

    def pump(until):
        if until > done[0]:
            start = done[0]
            loop(until - start, lambda i: tick(i + start))
            done[0] = until

    def pick(piece, seg):
        lanes = slice(WIDE * piece, WIDE * piece + WIDE)
        return jnp.where(seg > 0.5, mods[1:2, lanes], mods[0:1, lanes])

    def by_video(piece, value, seg):
        lanes = slice(WIDE * piece, WIDE * piece + WIDE)
        later = jnp.sum(value * seg, axis=0, keepdims=True)
        every = jnp.sum(value, axis=0, keepdims=True)
        gm[0:1, lanes] = gm[0:1, lanes] + (every - later)
        gm[1:2, lanes] = gm[1:2, lanes] + later

    def through(values_at, blocks, emit, grouped=False):
        for n, (values, block) in enumerate(zip(values_at, blocks)):
            have(("w", block))

            def tile(cols, n=n, values=values, block=block):
                part = nt(values[...], weight(block)[cols, :])
                if n > 0:
                    part = part + work[:, cols]
                if n == len(blocks) - 1:
                    xin[:, cols] = to_low(part)
                else:
                    work[:, cols] = part

            each_cols(tile)
            release(block)
        if grouped:
            xin[...] = to_low(linear(regroup(True), xin[...]))
        turn_back(emit)

    def turn_back(emit):
        each_cols(lambda cols: emit(cols, linear(xin[...], turn[:, cols])))

    def emit_work(cols, value):
        work[:, cols] = value

    def emit_grad(cols, value):
        grad[:, cols] = to_low(value)

    def norm_back(grad_in, tilt, at, rows):
        slope_in = grad_in * tilt
        hat = wide32(xhat[at, rows, :])
        first_mean = jnp.mean(slope_in, axis=-1, keepdims=True)
        second_mean = jnp.mean(slope_in * hat, axis=-1, keepdims=True)
        return rstd[at, rows, 0:1] * (slope_in - first_mean - hat * second_mean)

    gm[...] = jnp.zeros_like(gm)
    have(0)
    have(12)
    have(18)
    have(19)
    gm[0:8, 8 * WIDE : 9 * WIDE] = work[0:8]
    stream[...] = wide32(xin[...])
    for k in range(4):
        have(1 + k)
    pump(2)
    for k in range(4):
        have(14 + k % 2 if k < 2 else ("slope", k))
        have(("w", 11 + 2 * k))

        def tile(cols, k=k):
            value = nt(right[0], weight(11 + 2 * k)[cols, :]) * wide32(slope[k % 2, :, cols])
            right[1 + k, :, cols] = to_low(value)

        each_cols(tile)
        release(11 + 2 * k)
        if k < 2:
            copy = pltpu.make_async_copy(slope_i.at[k + 2], slope.at[k % 2], in_sem.at[14 + k])
            copy.start()
            fetches["slope", k + 2] = copy
        have(("w", 10 + 2 * k))

        def tile(cols, k=k):
            part = nt(right[1 + k], weight(10 + 2 * k)[cols, :])
            if k > 0:
                part = part + work[:, cols]
            if k < 3:
                work[:, cols] = part
            else:
                xin[:, cols] = to_low(part)

        each_cols(tile)
        release(10 + 2 * k)
        pump(k + 3)
    turn_back(emit_work)
    have(16)
    have(17)
    fetch(20, qc_i, qkv.at[0])
    fetch(21, mem_i.at[0], mem.at[0])
    fetch(22, mem_i.at[1], mem.at[1])
    fetch(23, xhat_i.at[2], xhat.at[0])
    fetch(24, rstd_i.at[2], rstd.at[0])

    def after_mlp(rows):
        seg = seg_in[0, rows, 0:1]
        value = work[rows, :]
        by_video(6, value, seg)
        by_video(7, value * wide32(xhat[1, rows, :]), seg)
        value = stream[rows, :] + norm_back(value, 1.0 + pick(7, seg), 1, rows)
        stream[rows, :] = value
        right[5, rows, :] = to_low(value)

    each_rows(32, after_mlp)

    fetch(25, xhat_i.at[1], xhat.at[1])
    fetch(26, rstd_i.at[1], rstd.at[1])
    through([right.at[5]], [9], emit_grad)
    right[6] = jnp.zeros_like(right[6])
    dmem[...] = jnp.zeros_like(dmem)
    for name in (13, 20, 21, 22, 23, 24):
        have(name)

    def cross_heads(h):
        text_heads_backward(
            h, qkv.at[0], mem.at[0], mem.at[1], grad, right.at[6], dmem.at[0], dmem.at[1],
            cross_bias(), cross_rows(seg_in),
        )

    for part in range(4):
        loop(2, lambda h: cross_heads(h + 2 * part))
        pump(7 + (part + 1) // 2)

    def dmem_part(zp, yp):
        return dmem.at[zp // 2, pl.ds(pl.multiple_of(TEXT * (zp % 2 * 2 + yp), 16), TEXT)]

    def x_over(zp):
        return remote(dmem_part(zp, 1 - y), text.at[zp], x_send.at[zp], x_recv.at[zp], device(x, c, 1 - y, z))

    def x_copy(k):
        return remote(text.at[(z + k) % 4], text_at.at[k - 1], x_send.at[3 + k], x_recv.at[3 + k], near[k - 1])

    for zp in range(4):
        x_over(zp).start()
    fetch(27, qkvt_i.at[0], qkv.at[0])
    fetch(28, qkvt_i.at[1], qkv.at[1])
    fetch(29, qkvt_i.at[2], qkv.at[2])
    fetch(30, branch_i.at[1], branch)
    through([right.at[6]], [8], emit_work)
    gains[0] = jnp.zeros_like(gains[0])
    have(30)

    def after_cross(rows):
        seg = seg_in[0, rows, 0:1]
        value = work[rows, :]
        gains[0, 0:1, :] = gains[0, 0:1, :] + jnp.sum(value * wide32(xhat[0, rows, :]), axis=0, keepdims=True)
        value = stream[rows, :] + norm_back(value, gain[0:1, :], 0, rows)
        stream[rows, :] = value
        by_video(5, value * wide32(branch[rows, :]), seg)
        right[7, rows, :] = to_low(value * pick(5, seg))

    each_rows(32, after_cross)

    def g_copy(at, to):
        return remote(gains.at[min(at, 3)], gain_at.at[at], g_send.at[at], g_recv.at[at], to)

    g_copy(0, twin).start()
    fetch(31, branch_i.at[0], branch)
    fetch(32, xhat_i.at[0], xhat.at[0])
    fetch(33, rstd_i.at[0], rstd.at[0])
    pump(10)

    through([right.at[7]], [7], emit_grad)
    grad[...] = to_low(linear(regroup(False), grad[...]))
    bias[...] = temporal_bias(seg_in, seg_row)
    for j in range(3):
        right[8 + j] = jnp.zeros_like(right[8 + j])
    for name in (25, 26, 27, 28, 29):
        have(name)

    def temporal_heads(h):
        heads_backward(
            h, qkv.at[0], qkv.at[1], qkv.at[2], grad, right.at[8], right.at[9], right.at[10],
            HALVES, jnp.concatenate([bias[...]] * 4), None,
        )

    loop(4, temporal_heads)
    pump(11)
    g_copy(0, twin).wait_recv()
    gains[1] = gains[0] + gain_at[0]
    g_copy(1, first).start()
    loop(4, lambda h: temporal_heads(h + 4))
    pump(12)
    g_copy(1, first).wait_recv()
    gains[2] = gains[1] + gain_at[1]
    g_copy(2, second).start()
    for zp in range(4):
        x_over(zp).wait_recv()
        text[zp] = to_low(wide32(dmem_part(zp, y)[...]) + wide32(text[zp]))
    for k in (1, 2, 3):
        x_copy(k).start()
    for j in range(3):
        fetch(34 + j, qkvs_i.at[j], qkv.at[j])
    through([right.at[8], right.at[9], right.at[10]], [4, 5, 6], emit_work, True)
    have(31)

    def after_temporal(rows):
        seg = seg_in[0, rows, 0:1]
        value = work[rows, :]
        by_video(3, value, seg)
        by_video(4, value * wide32(xhat[1, rows, :]), seg)
        value = stream[rows, :] + norm_back(value, 1.0 + pick(4, seg), 1, rows)
        stream[rows, :] = value
        by_video(2, value * wide32(branch[rows, :]), seg)
        right[1, rows, :] = to_low(value * pick(2, seg))

    each_rows(32, after_temporal)

    through([right.at[1]], [3], emit_grad)

    def a_copy(k):
        to = (b + k) % 8
        part = grad.at[pl.ds(pl.multiple_of(32 * to, 32), 32)]
        return remote(part, back.at[b], a_send.at[k - 1], a_recv.at[k - 1], peers[k - 1])

    def a_wait(k):
        of = (b + 8 - k) % 8
        remote(grad.at[pl.ds(0, 32)], back.at[of], a_send.at[k - 1], a_recv.at[k - 1], peers[k - 1]).wait_recv()

    for k in range(1, 8):
        a_copy(k).start()
    pump(13)
    for k in (1, 2, 3):
        x_copy(k).wait_recv()
    text_sum[...] = to_low(wide32(text[z]) + wide32(text_at[0]) + wide32(text_at[1]) + wide32(text_at[2]))

    def cap_fetch(n):
        quarter = [1 - c, 3 - c, c, 2 + c][n]
        lanes = pl.ds(pl.multiple_of(QUARTER * quarter, 128), QUARTER)
        return pltpu.make_async_copy(caption_i.at[:, :, lanes], cap.at[n % 2], cap_sem.at[n % 2])

    over_x = across[1]
    quarters = [x * 2 + c, (1 - x) * 2 + c, x * 2 + 1 - c, (1 - x) * 2 + 1 - c]

    def c_copy(n):
        from_ref, to_ref, to = (
            (cap_out.at[0], cap_in.at[0], twin),
            (cap_out.at[1], cap_in.at[1], twin),
            (cap_own.at[1 - x], cap_at, over_x),
            (cap_own.at[x], caption_o.at[quarters[0]], over_x),
            (cap_own.at[x], caption_o.at[quarters[0]], twin),
            (caption_o.at[quarters[1]], caption_o.at[quarters[1]], twin),
        )[n]
        return remote(from_ref, to_ref, c_send.at[n], c_recv.at[n], to)

    cap_fetch(0).start()
    cap_fetch(1).start()
    for n in range(4):
        cap_fetch(n).wait()
        part = linear(text_sum[:, 0:L], cap[n % 2, 0]) + linear(text_sum[:, 128 : 128 + L], cap[n % 2, 1])
        if n < 2:
            cap_out[n] = to_low(part)
            c_copy(n).start()
            cap_fetch(n + 2).start()
        else:
            cap_own[n - 2] = to_low(part)
    back[b] = grad[pl.ds(pl.multiple_of(32 * b, 32), 32)]
    pump(14)
    g_copy(2, second).wait_recv()
    gains[3] = gains[2] + gain_at[2]
    for k in (1, 2, 3):
        g_copy(2 + k, near[k - 1]).start()
    for j in range(3):
        right[2 + j] = jnp.zeros_like(right[2 + j])
    for name in (32, 33, 34, 35, 36):
        have(name)
    for k in range(1, 8):
        a_wait(k)
    for k in range(8):
        for f in range(2):
            gframe[128 * f + 16 * k : 128 * f + 16 * k + 16, :] = back[k, 16 * f : 16 * f + 16, :]

    def spatial_heads(h):
        heads_backward(
            h, qkv.at[0], qkv.at[1], qkv.at[2], gframe, right.at[2], right.at[3], right.at[4], HALVES, None, None
        )

    loop(4, spatial_heads)
    pump(15)
    for n in range(2):
        c_copy(n).wait_recv()
        cap_own[n] = to_low(wide32(cap_own[n]) + wide32(cap_in[n]))
    c_copy(2).start()
    loop(4, lambda h: spatial_heads(h + 4))
    pump(16)
    through([right.at[2], right.at[3], right.at[4]], [0, 1, 2], emit_work)
    pump(17)
    for k in range(1, 8):
        a_copy(k).wait_send()

    def after_spatial(i):
        rows = pl.ds(pl.multiple_of(16 * i, 16), 16)
        seg = seg_in[1, rows, 0:1]
        value = work[rows, :]
        by_video(0, value, seg)
        by_video(1, value * wide32(xhat[0, rows, :]), seg)
        value = to_low(norm_back(value, 1.0 + pick(1, seg), 0, rows))
        back[i % 8, pl.ds(pl.multiple_of(16 * (i // 8), 16), 16), :] = value

    loop(16, after_spatial)

    def branch_part(of):
        return branch.at[pl.ds(pl.multiple_of(32 * of, 32), 32)]

    def u_copy(k):
        to = (b + k) % 8
        return remote(back.at[to], branch_part(b), u_send.at[k - 1], u_recv.at[k - 1], peers[k - 1])

    def u_wait(k):
        of = (b + 8 - k) % 8
        remote(back.at[0], branch_part(of), u_send.at[k - 1], u_recv.at[k - 1], peers[k - 1]).wait_recv()

    def m_copy(k):
        to = (b + k) % 8
        return remote(mod_out.at[to], mod.at[b], m_send.at[k - 1], m_recv.at[k - 1], peers[k - 1])

    def m_wait(k):
        of = (b + 8 - k) % 8
        remote(mod_out.at[0], mod.at[of], m_send.at[k - 1], m_recv.at[k - 1], peers[k - 1]).wait_recv()

    for k in range(1, 8):
        u_copy(k).start()
    branch[pl.ds(pl.multiple_of(32 * b, 32), 32), :] = back[b]
    for k in range(8):
        tiles = [
            gm[row : row + 1, 1280 * k + 128 * tile : 1280 * k + 128 * tile + 128]
            for row in range(2)
            for tile in range(MOD_TILES)
        ]
        mod_out[k] = to_low(jnp.concatenate(tiles + [jnp.zeros((32 - 2 * MOD_TILES, 128), jnp.float32)]))
    for k in range(1, 8):
        m_copy(k).start()
    mod[b] = mod_out[b]
    pump(18)
    c_copy(2).wait_recv()
    cap_own[x] = to_low(wide32(cap_own[x]) + wide32(cap_at[...]))
    c_copy(3).start()
    c_copy(4).start()
    keep_quarter = pltpu.make_async_copy(cap_own.at[x], caption_o.at[quarters[0]], cap_sem.at[0])
    keep_quarter.start()
    pump(20)
    for k in range(1, 8):
        m_wait(k)
    summed = wide32(mod[0])
    for k in range(1, 8):
        summed = summed + wide32(mod[k])
    own = x * 2 + c
    seqs[own, 0:32] = to_low(summed)
    seqs[own, 32:64] = cond_in[...]
    places = [x * 2 + 1 - c, (1 - x) * 2 + c, (1 - x) * 2 + 1 - c]

    def q_copy(k, at):
        return remote(seqs.at[own], seqs.at[at], q_send.at[k], q_recv.at[k], across[k])

    for k in range(3):
        q_copy(k, own).start()
    pump(22)
    for k in range(1, 8):
        u_wait(k)
    xin[...] = to_low(stream[...] + wide32(branch[...]))
    gtok[...] = to_low(linear(swap_rows(), xin[...]))
    for k in (1, 2, 3):
        g_copy(2 + k, near[k - 1]).wait_recv()
    gain_o[...] = gains[3] + gain_at[3] + gain_at[4] + gain_at[5]
    pump(24)
    c_copy(3).wait_recv()
    c_copy(5).start()
    pump(BLOCKS + 10)
    c_copy(4).wait_recv()
    c_copy(5).wait_recv()
    for n in range(6):
        c_copy(n).wait_send()
    keep_quarter.wait()
    for k in range(3):
        q_copy(k, places[k]).wait_recv()
    mod_o[...] = seqs[...]

    for now in (BLOCKS - 2, BLOCKS - 1):
        for l in range(2):
            copy0(now, l).wait_send()
            copy1(now, l).wait_send()
        copy2(now).wait_send()
        z_three(now).wait_send()
        share_copy(now).wait()

        @pl.when(middle)
        def _(now=now):
            z_two(now).wait_send()

    for k in range(1, 8):
        u_copy(k).wait_send()
        m_copy(k).wait_send()
        x_over(k - 1).wait_send() if k < 5 else x_copy(k - 4).wait_send()
    for k in range(3):
        q_copy(k, own).wait_send()
    for at, to in enumerate([twin, first, second] + near):
        g_copy(at, to).wait_send()


QUARTER = 1024
WEIGHT_ORDER = (11, 10, 13, 12, 15, 14, 17, 16, 9, 8, 7, 4, 5, 6, 3, 0, 1, 2)


def backward(*operands):
    low, full = jnp.bfloat16, jnp.float32
    dma = pltpu.SemaphoreType.DMA
    outs = [
        ((BLOCKS, WINDOW, WIDE), full),
        ((ROWS, WIDE), low),
        ((8, WIDE), full),
        ((4, TEXT, QUARTER), low),
        ((4, 64, 128), low),
    ]
    vmem = [
        ((2, WIDE, WIDE), low),
        ((4, WIDE, ROWS), low),
        ((11, ROWS, WIDE), low),
        ((3, ROWS, WIDE), low),
        ((2, ROWS, WIDE), low),
        ((2, ROWS, 128), full),
        ((ROWS, WIDE), low),
        ((2, ROWS, WIDE), low),
        ((8, MOD), full),
        ((8, WIDE), full),
        ((128, 128), full),
        ((ROWS, WIDE), full),
        ((ROWS, WIDE), full),
        ((ROWS, WIDE), low),
        ((ROWS, WIDE), low),
        ((8, MOD), full),
        ((2, WIDE, KEYS), low),
        ((2, WIDE, KEYS), low),
        ((4, TEXT, KEYS), low),
        ((3, TEXT, KEYS), low),
        ((TEXT, KEYS), low),
        ((2, 2, L, QUARTER), low),
        ((2, TEXT, QUARTER), low),
        ((2, TEXT, QUARTER), low),
        ((2, TEXT, QUARTER), low),
        ((TEXT, QUARTER), low),
        ((8, 32, 128), low),
        ((8, 32, 128), low),
        ((4, 64, 128), low),
        ((4, 8, WIDE), full),
        ((6, 8, WIDE), full),
        ((ROWS, WIDE), low),
        ((8, 32, WIDE), low),
        ((2, 4, LINE, WIDE), low),
        ((4, 4, LINE, WIDE), low),
        ((2, 4, LINE, WIDE), low),
        ((4, 2, LINE, WIDE), low),
        ((2, LINE, WIDE), low),
        ((4, LINE, WIDE), low),
        ((2, LINE, WIDE), full),
        ((4, LINE, WIDE), low),
        ((4, PAIR, WIDE), low),
        ((2, PAIR, WIDE), low),
        ((4, PAIR, WIDE), low),
        ((2, PAIR, WIDE), low),
        ((4, WINDOW, WIDE), low),
        ((2, WINDOW, WIDE), full),
    ]
    return pl.pallas_call(
        backward_kernel,
        out_shape=[jax.ShapeDtypeStruct(*shape) for shape in outs],
        in_specs=[ANY] * 16 + [IN_VMEM] * 4,
        out_specs=[ANY] + [IN_VMEM] * 2 + [ANY, IN_VMEM],
        scratch_shapes=[pltpu.VMEM(*shape) for shape in vmem]
        + [
            dma((40,)), dma((2,)), dma((2, 4)), dma((4, 4)), dma((2, 2)), dma((4, 2)), dma((2,)), dma((4,)),
            dma((3, 4)), dma((3, 4)), dma((2,)), dma((7,)), dma((7,)), dma((7,)), dma((7,)), dma((7,)), dma((7,)),
            dma((7,)), dma((7,)), dma((3,)), dma((3,)), dma((6,)), dma((6,)), dma((2,)), dma((6,)), dma((6,)), dma((1,)),
        ],
        compiler_params=pltpu.CompilerParams(
            collective_id=1, has_side_effects=True, vmem_limit_bytes=63 * MIB
        ),
        name="backward",
    )(*operands)


def finish_kernel(
    spread, caption_in, mod_in, gain_in,
    ada_o, bias_o, spatial_o, spatial_out_o, temporal_o, temporal_out_o, gain_o, query_o, caption_o, cross_o, hidden_o,
    hidden_out_o,
):
    seq, blk = lax.axis_index("seq"), lax.axis_index("blk")

    def share(t):
        return pltpu.roll(spread[t], (WINDOW - 4 * (blk // 2)) % WINDOW, 0)[0:SHARD]

    for j in range(3):
        lanes = slice(WIDE * j, WIDE * j + WIDE)
        spatial_o[:, lanes] = share(15 + j)
        temporal_o[:, lanes] = share(11 + j)
    spatial_out_o[...] = share(14)
    temporal_out_o[...] = share(10)
    query_o[...] = share(9)
    cross_o[...] = share(8)
    hidden = [share(4 + k) for k in range(4)]
    hidden_o[...] = jnp.zeros_like(hidden_o)
    for k, natural, placed in hidden_places():
        move_lanes(hidden_o, hidden[k], placed, natural, 4 * WIDE)
    for k in range(4):
        hidden_out_o[SHARD * k : SHARD * k + SHARD, :] = share(k)
    gain_o[...] = pltpu.roll(gain_in[...], (WIDE - SHARD * (seq * 8 + blk)) % WIDE, 1)[0:1, 0:SHARD]
    for q in range(4):
        caption_o[:, QUARTER * q : QUARTER * q + QUARTER] = wide32(caption_in[q])
    part = MOD // 8
    mods, conds = [], []
    for pack in range(4):
        rows = wide32(mod_in[pack])
        for video in range(2):
            first = MOD_TILES * video
            mods.append(jnp.concatenate([rows[first + i : first + i + 1] for i in range(MOD_TILES)], axis=1))
            first = 32 + WIDE // 128 * video
            conds.append(jnp.concatenate([rows[first + i : first + i + 1] for i in range(WIDE // 128)], axis=1))
    mods = pltpu.roll(jnp.concatenate(mods), (MOD_WIN - 16 * blk) % MOD_WIN, 1)[:, :part]
    bias_o[...] = jnp.sum(mods, axis=0, keepdims=True)
    ada_o[...] = tn(to_low(mods), to_low(jnp.concatenate(conds)))


def finish(spread, caption, mod, gain):
    full = jnp.float32
    outs = [
        (MOD // 8, WIDE), (1, MOD // 8), (SHARD, 3 * WIDE), (SHARD, WIDE), (SHARD, 3 * WIDE), (SHARD, WIDE),
        (1, SHARD), (SHARD, WIDE), (TEXT, 4 * QUARTER), (SHARD, WIDE), (SHARD, 4 * WIDE), (4 * SHARD, WIDE),
    ]
    return pl.pallas_call(
        finish_kernel,
        out_shape=[jax.ShapeDtypeStruct(shape, full) for shape in outs],
        in_specs=[IN_VMEM] * 4,
        out_specs=[IN_VMEM] * len(outs),
        compiler_params=pltpu.CompilerParams(vmem_limit_bytes=60 * MIB),
        name="finish",
    )(spread, caption, mod, gain)


TURN = np.arange(WIDE)[None, :] == (
    np.arange(WIDE).reshape(2, 2, 4, 2, SHARD).transpose(1, 0, 3, 2, 4).reshape(-1)
)[:, None]


def shards(
    tokens,
    segments,
    timesteps,
    caption,
    cotangent,
    ada_weight,
    ada_bias,
    spatial_in,
    spatial_out,
    temporal_in,
    temporal_out,
    cross_gain,
    cross_query,
    caption_proj,
    cross_out,
    hidden_in,
    hidden_out,
):
    frame_seg = segments[0]
    blk = lax.axis_index("blk")
    conditioning = to_low(jax.nn.silu(time_embedding(timesteps[0], WIDE)))
    cond_in = jnp.pad(conditioning.reshape(2 * WIDE // 128, 128), ((0, 32 - 2 * WIDE // 128), (0, 0)))
    frames = frame_seg.astype(jnp.float32)
    own_frames = lax.dynamic_slice(frames, (2 * blk,), (2,))
    seg_in = jnp.broadcast_to(
        jnp.stack(
            [jnp.repeat(frames, 16), jnp.repeat(own_frames, 128), jnp.tile(jnp.repeat(frames, 8), 2)]
        )[:, :, None],
        (3, ROWS, 128),
    )
    seg_row = jnp.broadcast_to(jnp.repeat(frames, 8)[None], (8, 128))
    turn = jnp.asarray(TURN, jnp.bfloat16)
    wide, out, *kept = forward(
        spatial_in,
        spatial_out,
        temporal_in,
        temporal_out,
        cross_query,
        cross_out,
        hidden_in,
        hidden_out,
        tokens.reshape(ROWS, WIDE),
        jnp.pad(cross_gain[None], ((0, 7), (0, 0))),
        jnp.pad(conditioning, ((0, 14), (0, 0))),
        ada_bias[None],
        seg_in,
        seg_row,
        cotangent.reshape(ROWS, WIDE),
        turn,
        ada_weight.T,
        caption[0],
        caption_proj.T,
    )
    spread, grad_tokens, grad_gain, grad_text, grad_mod = backward(
        wide, *kept, caption[0], seg_in, seg_row, turn, cond_in
    )
    (
        grad_ada,
        grad_bias,
        grad_sin,
        grad_sout,
        grad_tin,
        grad_tout,
        grad_gain,
        grad_query,
        grad_caption,
        grad_cout,
        grad_hin,
        grad_hout,
    ) = finish(spread, grad_text, grad_mod, grad_gain)
    return (
        out.reshape(tokens.shape),
        grad_tokens.reshape(tokens.shape),
        grad_ada.T,
        grad_bias[0],
        grad_sin,
        grad_sout,
        grad_tin,
        grad_tout,
        grad_gain[0],
        grad_query,
        grad_caption.T,
        grad_cout,
        grad_hin,
        grad_hout,
    )


def solution(mesh):
    fast = dict(mesh.shape) == {"seq": 4, "blk": 8}
    return jax.shard_map(
        shards if fast else general_shards,
        mesh=mesh,
        in_specs=(
            P("seq", "blk", None, None),
            P("seq", None),
            P("seq", None),
            P("seq", None, None, None),
            P("seq", "blk", None, None),
            P(None, "blk"),
            P("blk"),
            P(("seq", "blk"), None),
            P(("seq", "blk"), None),
            P(("seq", "blk"), None),
            P(("seq", "blk"), None),
            P(("seq", "blk")),
            P(("seq", "blk"), None),
            P(None, "blk"),
            P(("seq", "blk"), None),
            P(("seq", "blk"), None),
            P(("seq", "blk"), None),
        ),
        out_specs=(
            P("seq", "blk", None, None),
            P("seq", "blk", None, None),
            P(None, "blk"),
            P("blk"),
            P(("seq", "blk"), None),
            P(("seq", "blk"), None),
            P(("seq", "blk"), None),
            P(("seq", "blk"), None),
            P(("seq", "blk")),
            P(("seq", "blk"), None),
            P(None, "blk"),
            P(("seq", "blk"), None),
            P(("seq", "blk"), None),
            P(("seq", "blk"), None),
        ),
        check_vma=False,
    )
```

profile of v0, /device:TPU:7, one launch (start us, length us, event | category | flops | bytes accessed | tf_op | source)
XLA Modules:
  0.0 543.4 jit_solution(10396346777829595385)
XLA Ops:
  0.6 0.7 convert_bitcast_fusion
  1.3 0.7 fusion.1
  2.0 0.1 dynamic-slice_bitcast_fusion
  2.0 0.1 broadcast_in_dim.32
  2.1 1.2 pad.12.gain_one
  3.4 1.3 broadcast_in_dim.30.ada_bias
  4.6 0.2 multiply_cosine_fusion
  4.8 0.1 fusion
  4.9 0.1 broadcast_in_dim.33
  5.0 0.1 tile.7
  5.1 0.6 broadcast_in_dim.35.seg_row
  5.7 0.1 broadcast_in_dim.31
  5.7 0.1 stack_reshape.6
  5.9 0.6 pad.14.cond_in
  6.5 0.6 pad.13.cond
  7.1 0.9 broadcast_in_dim.34.seg_in
  8.0 255.5 %forward.1 = (bf16[18,1152,1152]{2,1,0:T(8,128)(2,1)}, bf16[256,1152]{1,0:T(8,128)(2,1)}, bf16[11,1152,256]{2,1,0:T(8,128)(2,1)}, bf16[3,256,1152]{2,1,0:T(8,128...) custom-call(bf16[36,3456]{1,0:T(8,128)(2,1)} %spatial_in.1, ...), custom_call_target="tpu_custom_call" | custom-call | tf_op jit(solution)/shard_map/forward/pallas_call | solution.py:1292
  263.5 266.3 %backward.1 = (f32[18,48,1152]{2,1,0:T(8,128)}, bf16[256,1152]{1,0:T(8,128)(2,1)}, f32[8,1152]{1,0:T(8,128)}, bf16[4,288,1024]{2,1,0:T(8,128)(2,1)}, bf16[4,64,128]{2,1,0:T(8,128)(2,1)}) custom-call(bf16[18,1152,1152]{2,1,0:T(8,128)(2,1)} %get-tuple-element.48.wide, bf16[11,1152,256]{2,1,0:T(8,128)(2,1)} %get-tuple-element.49.left_i, ...), custom_call_target="tpu_custom_call" | custom-call | tf_op jit(solution)/shard_map/backward/pallas_call | solution.py:2048
  529.8 0.0 copy-start
  529.8 0.0 copy-start.1
  529.8 10.2 %finish.1 = (f32[1296,1152]{1,0:T(8,128)}, f32[1,1296]{1,0:T(1,128)}, f32[36,3456]{1,0:T(8,128)}, f32[36,1152]{1,0:T(8,128)}, f32[36,3456]{1,0:T(8,128)}, /*inde...) custom-call(f32[18,48,1152]{2,1,0:T(8,128)} %get-tuple-element.64.sp, ...), custom_call_target="tpu_custom_call" | custom-call | tf_op jit(solution)/shard_map/finish/pallas_call | solution.py:2113
  540.0 1.3 reduce
  541.3 0.0 copy-done
  541.3 0.8 copy.34
  542.1 0.0 copy-done.1
  542.1 0.8 copy.35
  (5 shorter events, 0.0 us)
Async XLA Ops:
  529.8 11.5 %copy-start = (bf16[256,1152]{1,0:T(8,128)(2,1)S(1)}, bf16[256,1152]{1,0:T(8,128)(2,1)}, u32[]{:S(2)}) copy-start(bf16[256,1152]{1,0:T(8,128)(2,1)} %get-tuple-element.47) | copy-start | bytes 1769476
  529.8 12.3 %copy-start.1 = (bf16[256,1152]{1,0:T(8,128)(2,1)S(1)}, bf16[256,1152]{1,0:T(8,128)(2,1)}, u32[]{:S(2)}) copy-start(bf16[256,1152]{1,0:T(8,128)(2,1)} %get-tuple-element.63) | copy-start | bytes 1769476
where the time goes:
time: 551 us; the launch traced here: 543 us
  Pallas kernels  532 us (97%)
  local copies, waits for them, and re-layouts  7.38 us (1%)
    pallas_call x1, Pallas kernels, backward(): pl.pallas_call(backward_kernel, out_shape=[jax.ShapeDtypeStruct(*shape) f...  266 us
    pallas_call x1, Pallas kernels, forward(): pl.pallas_call(forward_kernel, out_shape=[jax.ShapeDtypeStruct(*shape) fo...  255 us

commit v1 on v0

--- a/solution.py
+++ b/solution.py
@@ -560,8 +560,9 @@
     return probs if mask is None else probs * mask
 
 
-def chains(h, groups):
-    return [(window, rows, keys) for window in (head_window(h), head_window(h + H // 2)) for rows, keys in groups]
+def chains(h, groups, heads=2):
+    windows = [head_window(h + H // heads * i) for i in range(heads)]
+    return [(window, rows, keys) for window in windows for rows, keys in groups]
 
 
 def split_rows(values, jobs):
@@ -575,7 +576,7 @@
 
 
 def heads_forward(h, query, key, value, attn, groups, bias, mask):
-    jobs = chains(h, groups)
+    jobs = chains(h, groups, 4)
     scores = [nt(query[rows, lanes] * to_low(on), key[keys, lanes]) for (lanes, on), rows, keys in jobs]
     probs = split_rows(to_low(soft(jnp.concatenate(scores), bias, mask)), jobs)
     parts = [linear(prob, value[keys, lanes]) * on for prob, ((lanes, on), rows, keys) in zip(probs, jobs)]
@@ -584,7 +585,7 @@
 
 
 def text_heads_forward(h, query, key, value, attn, bias, mask):
-    jobs = chains(h, VIDEOS)
+    jobs = chains(h, VIDEOS, 4)
     scores = [linear(query[rows, lanes] * to_low(on), key[lanes, keys]) for (lanes, on), rows, keys in jobs]
     probs = split_rows(to_low(soft(jnp.concatenate(scores), bias, mask)), jobs)
     parts = [nt(prob, value[lanes, keys]) * on for prob, ((lanes, on), rows, keys) in zip(probs, jobs)]
@@ -618,9 +619,9 @@
     return jnp.where(col < L, 0.0, MASKED)
 
 
-def cross_rows(seg_in):
+def cross_rows(seg_in, heads=2):
     both = [1.0 - seg_in[0, 0:144, 0:1], seg_in[0, 112:256, 0:1]]
-    return jnp.concatenate(both + both)
+    return jnp.concatenate(both * heads)
 
 
 def move_lanes(to, value, from_start, to_start, width):
@@ -1024,9 +1025,9 @@
     def spatial_heads(h):
         heads_forward(h, qkvs.at[0], qkvs.at[1], qkvs.at[2], attnf, HALVES, None, None)
 
-    loop(4, spatial_heads)
+    loop(2, spatial_heads)
     poke()
-    loop(4, lambda h: spatial_heads(h + 4))
+    loop(2, lambda h: spatial_heads(h + 2))
     for k in (1, 2, 3):
         remote(gains.at[3], gain_at.at[2 + k], g_send.at[2 + k], g_recv.at[2 + k], near[k - 1]).wait_recv()
     gains[0 + 4] = gains[3] + gain_at[3] + gain_at[4] + gain_at[5]
@@ -1068,7 +1069,7 @@
         stream[rows, :] = value
         xin[rows, :] = to_low(normal(value, rows, 1) * (1.0 + pick(4, seg)) + pick(3, seg))
 
-    each_rows(32, after_spatial)
+    each_rows(64, after_spatial)
     save(branch.at[0], branch_o.at[0])
     save(xhat.at[1], xhat_o.at[1])
     save(rstd.at[1], rstd_o.at[1])
@@ -1092,12 +1093,12 @@
 
     def temporal_heads(h):
         heads_forward(
-            h, qkvt.at[0], qkvt.at[1], qkvt.at[2], attnf, HALVES, jnp.concatenate([bias[...]] * 4), None
+            h, qkvt.at[0], qkvt.at[1], qkvt.at[2], attnf, HALVES, jnp.concatenate([bias[...]] * 8), None
         )
 
-    loop(4, temporal_heads)
+    loop(2, temporal_heads)
     poke()
-    loop(4, lambda h: temporal_heads(h + 4))
+    loop(2, lambda h: temporal_heads(h + 2))
     xin[...] = to_low(linear(regroup(True), attnf[...]))
     turned(xin, 7)
     load(7)
@@ -1111,7 +1112,7 @@
         stream[rows, :] = value
         xin[rows, :] = to_low(normal(value, rows, 2) * gains[4, 0:1, :])
 
-    each_rows(32, after_temporal)
+    each_rows(64, after_temporal)
     save(branch.at[1], branch_o.at[1])
     save(xhat.at[2], xhat_o.at[2])
     save(rstd.at[2], rstd_o.at[2])
@@ -1131,11 +1132,11 @@
     attnf[...] = jnp.zeros_like(attnf)
 
     def cross_heads(h):
-        text_heads_forward(h, qc, mem.at[0], mem.at[1], attnf, cross_bias(), cross_rows(seg_in))
-
-    loop(4, cross_heads)
+        text_heads_forward(h, qc, mem.at[0], mem.at[1], attnf, cross_bias(), cross_rows(seg_in, 4))
+
+    loop(2, cross_heads)
     poke()
-    loop(4, lambda h: cross_heads(h + 4))
+    loop(2, lambda h: cross_heads(h + 2))
     xin[...] = attnf[...]
     turned(xin, 5)
     load(9)
@@ -1148,7 +1149,7 @@
         xin[rows, :] = to_low(normal(value, rows, 3) * (1.0 + pick(7, seg)) + pick(6, seg))
         gfour[rows, :] = to_low(wide32(cotp[rows, :]) * pick(8, seg))
 
-    each_rows(32, after_cross)
+    each_rows(64, after_cross)
     save(xhat.at[3], xhat_o.at[3])
     save(rstd.at[3], rstd_o.at[3])
     save(gfour, gfour_o)
@@ -1192,7 +1193,7 @@
         gate[0:1, :] = gate[0:1, :] + (every - later)
         gate[1:2, :] = gate[1:2, :] + later
 
-    each_rows(32, last)
+    each_rows(64, last)
     save(gate, gate_o)
     out[...] = to_low(linear(swap_rows(), xin[...]))
 

time: 551 us -> 550 us (level)
  no operation moved by 1% of the time
where the time goes in v1:
time: 550 us; the launch traced here: 542 us
  Pallas kernels  531 us (97%)
  local copies, waits for them, and re-layouts  7.38 us (1%)
    pallas_call x1, Pallas kernels, backward(): pl.pallas_call(backward_kernel, out_shape=[jax.ShapeDtypeStruct(*shape) f...  266 us
    pallas_call x1, Pallas kernels, forward(): pl.pallas_call(forward_kernel, out_shape=[jax.ShapeDtypeStruct(*shape) fo...  254 us

profile of v1, /device:TPU:7, one launch (start us, length us, event | category | flops | bytes accessed | tf_op | source)
XLA Modules:
  0.0 542.2 jit_solution(2307089080887294428)
XLA Ops:
  0.6 0.7 convert_bitcast_fusion
  1.3 0.7 fusion.1
  2.0 0.1 dynamic-slice_bitcast_fusion
  2.0 0.1 broadcast_in_dim.32
  2.1 1.2 pad.12.gain_one
  3.4 1.3 broadcast_in_dim.30.ada_bias
  4.6 0.2 multiply_cosine_fusion
  4.8 0.1 fusion
  4.9 0.1 broadcast_in_dim.33
  5.0 0.1 tile.7
  5.1 0.6 broadcast_in_dim.35.seg_row
  5.7 0.1 broadcast_in_dim.31
  5.7 0.1 stack_reshape.6
  5.9 0.6 pad.14.cond_in
  6.5 0.6 pad.13.cond
  7.1 0.9 broadcast_in_dim.34.seg_in
  8.0 254.3 %forward.1 = (bf16[18,1152,1152]{2,1,0:T(8,128)(2,1)}, bf16[256,1152]{1,0:T(8,128)(2,1)}, bf16[11,1152,256]{2,1,0:T(8,128)(2,1)}, bf16[3,256,1152]{2,1,0:T(8,128...) custom-call(bf16[36,3456]{1,0:T(8,128)(2,1)} %spatial_in.1, ...), custom_call_target="tpu_custom_call" | custom-call | tf_op jit(solution)/shard_map/forward/pallas_call | solution.py:1293
  262.3 266.4 %backward.1 = (f32[18,48,1152]{2,1,0:T(8,128)}, bf16[256,1152]{1,0:T(8,128)(2,1)}, f32[8,1152]{1,0:T(8,128)}, bf16[4,288,1024]{2,1,0:T(8,128)(2,1)}, bf16[4,64,128]{2,1,0:T(8,128)(2,1)}) custom-call(bf16[18,1152,1152]{2,1,0:T(8,128)(2,1)} %get-tuple-element.48.wide, bf16[11,1152,256]{2,1,0:T(8,128)(2,1)} %get-tuple-element.49.left_i, ...), custom_call_target="tpu_custom_call" | custom-call | tf_op jit(solution)/shard_map/backward/pallas_call | solution.py:2049
  528.6 0.0 copy-start
  528.7 0.0 copy-start.1
  528.7 10.2 %finish.1 = (f32[1296,1152]{1,0:T(8,128)}, f32[1,1296]{1,0:T(1,128)}, f32[36,3456]{1,0:T(8,128)}, f32[36,1152]{1,0:T(8,128)}, f32[36,3456]{1,0:T(8,128)}, /*inde...) custom-call(f32[18,48,1152]{2,1,0:T(8,128)} %get-tuple-element.64.sp, ...), custom_call_target="tpu_custom_call" | custom-call | tf_op jit(solution)/shard_map/finish/pallas_call | solution.py:2114
  538.8 1.3 reduce
  540.1 0.0 copy-done
  540.1 0.8 copy.34
  541.0 0.0 copy-done.1
  541.0 0.8 copy.35
  (5 shorter events, 0.0 us)
Async XLA Ops:
  528.6 11.5 %copy-start = (bf16[256,1152]{1,0:T(8,128)(2,1)S(1)}, bf16[256,1152]{1,0:T(8,128)(2,1)}, u32[]{:S(2)}) copy-start(bf16[256,1152]{1,0:T(8,128)(2,1)} %get-tuple-element.47) | copy-start | bytes 1769476
  528.7 12.3 %copy-start.1 = (bf16[256,1152]{1,0:T(8,128)(2,1)S(1)}, bf16[256,1152]{1,0:T(8,128)(2,1)}, u32[]{:S(2)}) copy-start(bf16[256,1152]{1,0:T(8,128)(2,1)} %get-tuple-element.63) | copy-start | bytes 1769476
